TPU v7x, 32 devices: a whole 2x2x4 slice. The times are simulated.
32 devices in a mesh: narrow: 4 (over y, core), wide: 8 (over z, x).
Axes of the slice: x: 2, y: 2, z: 4, core: 2. Of those that a mesh axis runs over, the one named last changes fastest.
Arguments:
- tokens: bfloat16 [4, 4, 1024, 384], P('narrow', None, 'wide'), may hold values from -6 to 6
- cotangent: bfloat16 [4, 4, 1024, 384], P('narrow', None, 'wide'), may hold values from -6 to 6
- emb_table: bfloat16 [4, 384], replicated, may hold values from -5 to 5
- ada_weight: bfloat16 [1, 384, 2304], replicated, may hold values from -0.3125 to 0.3125
- ada_bias: bfloat16 [1, 2304], replicated, may hold values from -3 to 3
- qkv_weight: bfloat16 [1, 384, 1152], replicated, may hold values from -0.3125 to 0.3125
- out_weight: bfloat16 [1, 384, 384], replicated, may hold values from -6 to 6
- out_bias: bfloat16 [1, 384], replicated, may hold values from -3 to 3
- up_weight: bfloat16 [1, 384, 1536], replicated, may hold values from -0.3125 to 0.3125
- up_bias: bfloat16 [1, 1536], replicated, may hold values from -3 to 3
- down_weight: bfloat16 [1, 1536, 384], replicated, may hold values from -0.15625 to 0.15625
- down_bias: bfloat16 [1, 384], replicated, may hold values from -3 to 3
- lead_class: int32 [4, 4], replicated, may hold values from 0 to 3
- group_count: int32 [4], replicated, may hold values from 3 to 4, as said below
Outputs:
- output: float32 [4, 4, 1024, 384], P('narrow', None, 'wide')
- grad_tokens: float32 [4, 4, 1024, 384], P('narrow', None, 'wide')
- grad_table: float32 [4, 384], replicated
- grad_ada_weight: float32 [1, 384, 2304], replicated
- grad_ada_bias: float32 [1, 2304], replicated
- grad_qkv_weight: float32 [1, 384, 1152], replicated
- grad_out_weight: float32 [1, 384, 384], replicated
- grad_out_bias: float32 [1, 384], replicated
- grad_up_weight: float32 [1, 384, 1536], replicated
- grad_up_bias: float32 [1, 1536], replicated
- grad_down_weight: float32 [1, 1536, 384], replicated
- grad_down_bias: float32 [1, 384], replicated
Inputs may be any that keep to these rules, and one draw needn't show every extreme that they name: `group_count`: half of the groups hold 4 live items and the others 4 - 1; a group's live items fill its first slots.
All inputs are finite; a program needn't handle non-finite values.
Results may differ from a plain program's by a relative error of at most 0.028.
Values may be sent and summed in bfloat16 or wider, within the bound.
A program may use at most 320 MiB of HBM per device.

v0:
```python
import jax
import jax.numpy as jnp
from jax import lax
from jax.sharding import PartitionSpec as P

HEADS = 6
HEAD_DIM = 64
LAYERS = 1


epsilon = 1e-06
highest = lax.Precision.HIGHEST
root_half = 0.7071067811865476
inverse_root_two_pi = 0.3989422804014327


def layer_norm(values):
    average = jnp.mean(values, axis=-1, keepdims=True)
    centred = values - average
    variance = jnp.mean(centred * centred, axis=-1, keepdims=True)
    inverse = lax.rsqrt(variance + epsilon)
    return (centred * inverse, inverse)


def norm_back(grad_normed, normed, inverse):
    first = jnp.mean(grad_normed, axis=-1, keepdims=True)
    second = jnp.mean(grad_normed * normed, axis=-1, keepdims=True)
    return inverse * (grad_normed - first - normed * second)


def gelu_exact(values):
    return 0.5 * values * (1.0 + jax.scipy.special.erf(values * root_half))


def gelu_slope(values):
    return 0.5 * (
        1.0 + jax.scipy.special.erf(values * root_half)
    ) + values * inverse_root_two_pi * jnp.exp(-0.5 * values * values)


def split_heads(values):
    return values.reshape(values.shape[0], values.shape[1], HEADS, values.shape[2] // HEADS)


def modulation_parts(silu_rows, ada_w, ada_b):
    mods = jnp.dot(silu_rows, ada_w.astype(jnp.float32), precision=highest) + ada_b.astype(
        jnp.float32
    )
    mods = mods.reshape(mods.shape[0], 6, -1)
    return [mods[:, index][:, None, :] for index in range(6)]


def before_attention(hidden, parts, qkv_low):
    normed, inverse = layer_norm(hidden)
    modulated = (normed * (1.0 + parts[1]) + parts[0]).astype(jnp.bfloat16)
    projected = jnp.einsum(
        "spd,df->spf", modulated, qkv_low, preferred_element_type=jnp.float32
    ).astype(jnp.bfloat16)
    width = hidden.shape[2]
    return (
        normed,
        inverse,
        modulated,
        projected[..., :width],
        projected[..., width : 2 * width],
        projected[..., 2 * width :],
    )


def after_attention(hidden, attended, parts, later):
    out_w, out_b, up_w, up_b, down_w, down_b = later
    branch = jnp.einsum(
        "spd,de->spe", attended, out_w, preferred_element_type=jnp.float32
    ) + out_b.astype(jnp.float32)
    middle = hidden + parts[2] * branch
    normed, inverse = layer_norm(middle)
    modulated = (normed * (1.0 + parts[4]) + parts[3]).astype(jnp.bfloat16)
    upward = jnp.einsum(
        "spd,df->spf", modulated, up_w, preferred_element_type=jnp.float32
    ) + up_b.astype(jnp.float32)
    activated = gelu_exact(upward).astype(jnp.bfloat16)
    feed = jnp.einsum(
        "spf,fd->spd", activated, down_w, preferred_element_type=jnp.float32
    ) + down_b.astype(jnp.float32)
    return (
        middle + parts[5] * feed,
        (branch, middle, normed, inverse, modulated, upward, activated, feed),
    )


def attention_forward(queries, keys_here, values_here):
    slots, rows, width = queries.shape
    scale = HEAD_DIM ** (-0.5)
    query_heads = split_heads(queries)
    running_max = jnp.full((slots, rows, HEADS), -1e30, jnp.float32)
    key_heads = split_heads(lax.all_gather(keys_here, "wide", axis=1, tiled=True))
    value_heads = split_heads(lax.all_gather(values_here, "wide", axis=1, tiled=True))
    scores = (
        jnp.einsum("sphe,snhe->sphn", query_heads, key_heads, preferred_element_type=jnp.float32)
        * scale
    )
    new_max = jnp.maximum(running_max, jnp.max(scores, axis=-1))
    weights = jnp.exp(scores - new_max[..., None])
    new_sum = jnp.sum(weights, axis=-1)
    mixed = jnp.einsum(
        "sphn,snhe->sphe",
        weights.astype(jnp.bfloat16),
        value_heads,
        preferred_element_type=jnp.float32,
    )
    total = mixed
    running_max, running_sum, total = (new_max, new_sum, total.reshape(slots, rows, width))
    attended = (
        (split_heads(total) / running_sum[..., None])
        .reshape(slots, rows, width)
        .astype(jnp.bfloat16)
    )
    return (attended, running_max + jnp.log(running_sum), None)


def attention_backward(queries, keys_here, values_here, grad_attended, log_total, delta):
    slots, rows, width = queries.shape
    scale = HEAD_DIM ** (-0.5)
    query_heads = split_heads(queries)
    grad_heads = split_heads(grad_attended)
    piece = (
        lax.all_gather(keys_here, "wide", axis=1, tiled=True),
        lax.all_gather(values_here, "wide", axis=1, tiled=True),
    )
    toward_key_heads = split_heads(piece[0])
    toward_value_heads = split_heads(piece[1])
    scores = (
        jnp.einsum(
            "sphe,snhe->sphn", query_heads, toward_key_heads, preferred_element_type=jnp.float32
        )
        * scale
    )
    probs = jnp.exp(scores - log_total[..., None])
    slope = jnp.einsum(
        "sphe,snhe->sphn", grad_heads, toward_value_heads, preferred_element_type=jnp.float32
    )
    grad_scores = (probs * (slope - delta[..., None])).astype(jnp.bfloat16)
    grad_queries = (
        jnp.einsum(
            "sphn,snhe->sphe", grad_scores, toward_key_heads, preferred_element_type=jnp.float32
        )
        * scale
    ).reshape(slots, rows, width)
    stats = (
        lax.all_gather(log_total, "wide", axis=1, tiled=True),
        lax.all_gather(delta, "wide", axis=1, tiled=True),
    )
    key_heads = split_heads(keys_here)
    value_heads = split_heads(values_here)
    piece = (
        lax.all_gather(queries, "wide", axis=1, tiled=True),
        lax.all_gather(grad_attended, "wide", axis=1, tiled=True),
    )
    piece_queries = split_heads(piece[0])
    piece_grads = split_heads(piece[1])
    piece_total = stats[0]
    piece_delta = stats[1]
    scores = (
        jnp.einsum("snhe,sphe->snhp", piece_queries, key_heads, preferred_element_type=jnp.float32)
        * scale
    )
    probs = jnp.exp(scores - piece_total[..., None])
    slope = jnp.einsum(
        "snhe,sphe->snhp", piece_grads, value_heads, preferred_element_type=jnp.float32
    )
    grad_scores = (probs * (slope - piece_delta[..., None])).astype(jnp.bfloat16)
    keys_total = (
        jnp.einsum(
            "snhp,snhe->sphe", grad_scores, piece_queries, preferred_element_type=jnp.float32
        )
        * scale
    ).reshape(slots, rows, width)
    values_total = jnp.einsum(
        "snhp,snhe->sphe",
        probs.astype(jnp.bfloat16),
        piece_grads,
        preferred_element_type=jnp.float32,
    ).reshape(slots, rows, width)
    return (
        grad_queries.astype(jnp.bfloat16),
        keys_total.astype(jnp.bfloat16),
        values_total.astype(jnp.bfloat16),
    )


def body(
    tokens,
    cotangent,
    emb_table,
    ada_weight,
    ada_bias,
    qkv_weight,
    out_weight,
    out_bias,
    up_weight,
    up_bias,
    down_weight,
    down_bias,
    lead_class,
    group_count,
):
    group = lax.axis_index("narrow")
    slot_count = tokens.shape[1]
    width = tokens.shape[3]
    table = emb_table.astype(jnp.float32)
    class_range = jnp.arange(table.shape[0], dtype=jnp.int32)
    classes_here = lax.dynamic_index_in_dim(lead_class, group, 0, keepdims=False)
    count_here = lax.dynamic_index_in_dim(group_count, group, 0, keepdims=False)
    live = (jnp.arange(slot_count, dtype=jnp.int32) < count_here).astype(jnp.float32)[:, None, None]
    embed_here = jnp.dot(
        (classes_here[:, None] == class_range[None, :]).astype(jnp.float32),
        table,
        precision=highest,
    )
    silu_here = embed_here * jax.nn.sigmoid(embed_here)
    hidden = tokens[0].astype(jnp.float32)
    layer = 0
    parts = modulation_parts(silu_here, ada_weight[layer], ada_bias[layer])
    later = (
        out_weight[layer],
        out_bias[layer],
        up_weight[layer],
        up_bias[layer],
        down_weight[layer],
        down_bias[layer],
    )
    normed, inverse, modulated, queries, keys_here, values_here = before_attention(
        hidden, parts, qkv_weight[layer]
    )
    attended, log_total, whole_pair = attention_forward(queries, keys_here, values_here)
    kept = [(hidden, parts, attended, log_total, whole_pair)]
    hidden, unused = after_attention(hidden, attended, parts, later)
    output = hidden * live
    grad = cotangent[0].astype(jnp.float32) * live
    grad_mods = [None] * LAYERS
    weight_grads = [None] * LAYERS
    for layer in reversed(range(LAYERS)):
        layer_input, parts, attended, log_total, whole_pair = kept[layer]
        later = (
            out_weight[layer],
            out_bias[layer],
            up_weight[layer],
            up_bias[layer],
            down_weight[layer],
            down_bias[layer],
        )
        normed, inverse, modulated, queries, keys_here, values_here = before_attention(
            layer_input, parts, qkv_weight[layer]
        )
        unused, inner = after_attention(layer_input, attended, parts, later)
        branch, middle, normed_mlp, inverse_mlp, modulated_mlp, upward, activated, feed = inner
        grad_feed = (grad * parts[5]).astype(jnp.bfloat16)
        grad_gate_mlp = jnp.sum(grad * feed, axis=1)
        grad_down_w = jnp.einsum(
            "spf,spd->fd", activated, grad_feed, preferred_element_type=jnp.float32
        )
        grad_down_b = jnp.sum(grad_feed.astype(jnp.float32), axis=(0, 1))
        grad_upward = (
            jnp.einsum(
                "spd,fd->spf", grad_feed, down_weight[layer], preferred_element_type=jnp.float32
            )
            * gelu_slope(upward)
        ).astype(jnp.bfloat16)
        grad_up_w = jnp.einsum(
            "spd,spf->df", modulated_mlp, grad_upward, preferred_element_type=jnp.float32
        )
        grad_up_b = jnp.sum(grad_upward.astype(jnp.float32), axis=(0, 1))
        grad_mod_mlp = jnp.einsum(
            "spf,df->spd", grad_upward, up_weight[layer], preferred_element_type=jnp.float32
        )
        grad_shift_mlp = jnp.sum(grad_mod_mlp, axis=1)
        grad_scale_mlp = jnp.sum(grad_mod_mlp * normed_mlp, axis=1)
        grad_middle = grad + norm_back(grad_mod_mlp * (1.0 + parts[4]), normed_mlp, inverse_mlp)
        grad_gate_attn = jnp.sum(grad_middle * branch, axis=1)
        grad_branch = (grad_middle * parts[2]).astype(jnp.bfloat16)
        grad_out_w = jnp.einsum(
            "spd,spe->de", attended, grad_branch, preferred_element_type=jnp.float32
        )
        grad_out_b = jnp.sum(grad_branch.astype(jnp.float32), axis=(0, 1))
        grad_attended = jnp.einsum(
            "spe,de->spd", grad_branch, out_weight[layer], preferred_element_type=jnp.float32
        ).astype(jnp.bfloat16)
        delta = jnp.sum(
            split_heads(grad_attended.astype(jnp.float32) * attended.astype(jnp.float32)), axis=-1
        )
        grad_queries, grad_keys, grad_values = attention_backward(
            queries, keys_here, values_here, grad_attended, log_total, delta
        )
        grad_projected = jnp.concatenate([grad_queries, grad_keys, grad_values], axis=-1)
        grad_qkv_w = jnp.einsum(
            "spd,spf->df", modulated, grad_projected, preferred_element_type=jnp.float32
        )
        grad_mod_attn = jnp.einsum(
            "spf,df->spd", grad_projected, qkv_weight[layer], preferred_element_type=jnp.float32
        )
        grad_shift_attn = jnp.sum(grad_mod_attn, axis=1)
        grad_scale_attn = jnp.sum(grad_mod_attn * normed, axis=1)
        grad = grad_middle + norm_back(grad_mod_attn * (1.0 + parts[1]), normed, inverse)
        local_mods = jnp.stack(
            [
                grad_shift_attn,
                grad_scale_attn,
                grad_gate_attn,
                grad_shift_mlp,
                grad_scale_mlp,
                grad_gate_mlp,
            ],
            axis=1,
        ).reshape(slot_count, 6 * width)
        grad_mods[layer] = lax.psum(local_mods, "wide")
        weight_grads[layer] = lax.psum(
            (grad_qkv_w, grad_out_w, grad_out_b, grad_up_w, grad_up_b, grad_down_w, grad_down_b),
            ("narrow", "wide"),
        )
    all_mods = lax.all_gather(
        jnp.stack(grad_mods, axis=0).astype(jnp.bfloat16), "narrow", axis=1, tiled=True
    ).astype(jnp.float32)
    all_classes = lead_class.reshape(-1)
    onehot_all = (all_classes[:, None] == class_range[None, :]).astype(jnp.float32)
    embed_all = jnp.dot(onehot_all, table, precision=highest)
    sigmoid_all = jax.nn.sigmoid(embed_all)
    silu_all = embed_all * sigmoid_all
    grad_ada_w = jnp.einsum("id,lie->lde", silu_all, all_mods, precision=highest)
    grad_ada_b = jnp.sum(all_mods, axis=1)
    grad_silu = jnp.einsum(
        "lie,lde->id", all_mods, ada_weight.astype(jnp.float32), precision=highest
    )
    grad_embed = grad_silu * (sigmoid_all + embed_all * sigmoid_all * (1.0 - sigmoid_all))
    grad_table = jnp.dot(onehot_all.T, grad_embed, precision=highest)
    stacked = [jnp.stack([weight_grads[0][member]], axis=0) for member in range(7)]
    return (
        output[None],
        grad[None],
        grad_table,
        grad_ada_w,
        grad_ada_b,
        stacked[0],
        stacked[1],
        stacked[2],
        stacked[3],
        stacked[4],
        stacked[5],
        stacked[6],
    )


def solution(mesh):
    in_specs = (
        P("narrow", None, "wide", None),
        P("narrow", None, "wide", None),
        P(),
        P(),
        P(),
        P(),
        P(),
        P(),
        P(),
        P(),
        P(),
        P(),
        P(),
        P(),
    )
    out_specs = (
        P("narrow", None, "wide", None),
        P("narrow", None, "wide", None),
        P(),
        P(),
        P(),
        P(),
        P(),
        P(),
        P(),
        P(),
        P(),
        P(),
    )
    return jax.shard_map(body, mesh=mesh, in_specs=in_specs, out_specs=out_specs, check_vma=False)
```

profile of v0, /device:TPU:9, one launch (start us, length us, event | category | flops | bytes accessed | tf_op | source)
XLA Modules:
  0.0 495.1 jit_solution(13261864830736711270)
XLA Ops:
  10.5 1.1 convert_reduce_fusion.1
  11.7 1.3 fusion.84
  13.1 2.2 convolution_convert_fusion
  18.4 1.2 copy.93
  21.0 55.9 %all-gather.9.cloned.1.call-done = bf16[4,1024,384]{2,1,0:T(8,128)(2,1)} async-done(((bf16[4,128,384]{2,1,0:T(8,128)(2,1)}), bf16[4,1024,384]{2,1,0:T(8,128)(2,1)}) %all-gather.9.cloned.1.call-update) | async-done | bytes 3145744 | tf_op jit(solution)/shard_map/all_gather | solution.py:96
  76.9 4.7 copy.92
  81.6 56.7 %all-gather.7.cloned.1.call-done = bf16[4,1024,384]{2,1,0:T(8,128)(2,1)} async-done(((bf16[4,128,384]{2,1,0:T(8,128)(2,1)}), bf16[4,1024,384]{2,1,0:T(8,128)(2,1)}) %all-gather.7.cloned.1.call-update) | async-done | bytes 3145744 | tf_op jit(solution)/shard_map/all_gather | solution.py:97
  138.2 4.6 copy.91
  142.9 4.0 bitcast_reduce_fusion
  146.9 2.1 fusion.7
  149.0 3.3 copy-done.1
  152.3 2.5 fusion.64
  155.8 2.4 fusion.137
  158.5 1.1 multiply_convert_fusion
  159.8 2.5 convert_reduce_fusion
  162.4 1.7 multiply_reduce_fusion
  164.1 3.0 convert_reduce_fusion.2
  167.1 1.4 convert_multiply_fusion.1
  168.6 2.0 copy.101
  171.5 1.2 copy.96
  172.7 2.3 copy.98
  175.1 1.2 reduce_sum.205
  176.3 11.7 %fusion.42 = bf16[4,6,64,128]{3,2,1,0:T(8,128)(2,1)} fusion(bf16[4,1024,6,64]{1,3,2,0:T(8,128)(2,1)} %bitcast.264, f32[4,6,1024,128]{3,2,1,0:T(8,128)} %copy-done.1, f32[4,128,6]{1,2,0:T(8,128)S(1)} %reduce_sum.205, f32[4,128,6]{1,2,0:T(8,128)S(1)} %log_add_fusion, bf16[4,1024,6,64]{1,3,2,0:T(8,128)(2,1)} %bitcast.272, bf16[4,128,6,64]{1,3,2,0:T(8,128)(2,1)S(1)} %bitcast.279), kind=kOutput, calls=%fused_computation.52 | convolution fusion | flops 821428224 | bytes 19685376 | tf_op jit(solution)/shard_map/sphn,snhe->sphe/dot_general | solution.py:144
  188.0 1.9 copy.106
  189.9 10.2 %all-gather.11.cloned.1.call-done = bf16[4,1024,384]{2,1,0:T(8,128)(2,1)} async-done(((bf16[4,128,384]{2,1,0:T(8,128)(2,1)}), bf16[4,1024,384]{2,1,0:T(8,128)(2,1)}) %all-gather.11.cloned.1.call-update) | async-done | bytes 3145744 | tf_op jit(solution)/shard_map/all_gather | solution.py:156
  200.2 4.7 copy.100
  204.9 22.7 %all_gather.26 = f32[4,1024,6]{1,2,0:T(8,128)S(1)} all-gather(f32[4,128,6]{1,2,0:T(8,128)S(1)} %log_add_fusion), channel_id=1, replica_groups=mesh['narrow'=4,'wide'=8] {'wide'}, dimensions={1}, use_global_device_ids=true | all-gather | bytes 110592 | tf_op jit(solution)/shard_map/all_gather | solution.py:150
  227.5 27.3 %all_gather.28 = f32[4,1024,6]{1,2,0:T(8,128)} all-gather(f32[4,128,6]{1,2,0:T(8,128)S(1)} %reduce_sum.205), channel_id=1, replica_groups=mesh['narrow'=4,'wide'=8] {'wide'}, dimensions={1}, use_global_device_ids=true | all-gather | bytes 110592 | tf_op jit(solution)/shard_map/all_gather | solution.py:151
  254.8 2.2 convolution_bitcast_fusion.4
  257.0 4.1 convolution_bitcast_fusion.1
  261.1 2.3 convolution_bitcast_fusion.2
  263.4 6.4 %fusion.143 = f32[4,6,128,1024]{3,2,1,0:T(8,128)} fusion(bf16[4,128,6,64]{1,3,2,0:T(8,128)(2,1)S(1)} %bitcast.276, bf16[4,1024,6,64]{1,3,2,0:T(8,128)(2,1)S(1)} %bitcast.266), kind=kOutput, calls=%fused_computation.181 | convolution fusion | flops 402653184 | bytes 16121856 | tf_op jit(solution)/shard_map/snhe,sphe->snhp/dot_general | solution.py:164
  269.9 4.6 copy.103
  274.5 8.0 %fusion.48 = bf16[4,6,64,128]{3,2,1,0:T(8,128)(2,1)S(1)} fusion(bf16[4,1024,6,64]{1,3,2,0:T(8,128)(2,1)} %bitcast.267, f32[4,6,128,1024]{3,2,1,0:T(8,128)} %fusion.143, f32[4,1024,6]{1,2,0:T(8,128)S(1)} %all_gather.26), kind=kOutput, calls=%fused_computation.54 | convolution fusion | flops 412286976 | bytes 16220160 | tf_op jit(solution)/shard_map/snhp,snhe->sphe/dot_general | solution.py:178
  282.5 12.5 %fusion.45 = bf16[4,6,64,128]{3,2,1,0:T(8,128)(2,1)} fusion(bf16[4,1024,6,64]{1,3,2,0:T(8,128)(2,1)} %bitcast.265, f32[4,6,128,1024]{3,2,1,0:T(8,128)} %fusion.143, f32[4,1024,6]{1,2,0:T(8,128)} %all_gather.28, f32[4,1024,6]{1,2,0:T(8,128)S(1)} %all_gather.26, bf16[4,128,6,64]{1,3,2,0:T(8,128)(2,1)S(1)} %bitcast.278, bf16[4,1024,6,64]{1,3,2,0:T(8,128)(2,1)} %bitcast.268), kind=kOutput, calls=%fused_computation.53 | convolution fusion | flops 821428224 | bytes 19857408 | tf_op jit(solution)/shard_map/snhp,snhe->sphe/dot_general | solution.py:173
  294.9 1.2 copy.107
  297.1 3.0 convolution_bitcast_fusion.3
  301.2 56.6 %all-reduce = (f32[1,384]{1,0:T(1,128)}, f32[1,1536]{1,0:T(1,128)}, f32[1,384]{1,0:T(1,128)}) all-reduce(f32[1,384]{1,0:T(1,128)S(1)} %stack.52, f32[1,1536]{1,0:T(1,128)S(1)} %stack.54, f32[1,384]{1,0:T(1,128)S(1)} %stack.56), channel_id=1, replica_groups=mesh['narrow'=4,'wide'=8] {'narrow','wide'}, use_global_device_ids=true, to_apply=%region_22.23 | all-reduce | flops 2304 | bytes 18432 | tf_op jit(solution)/shard_map/psum | solution.py:316
  357.8 2.4 fusion.81
  360.2 1.4 multiply_reduce_fusion.1
  361.7 25.5 %psum.56 = bf16[4,2304]{1,0:T(4,128)(2,1)S(1)} all-reduce(f32[4,2304]{1,0:T(4,128)S(1)} %bitcast.283), channel_id=1, replica_groups=mesh['narrow'=4,'wide'=8] {'wide'}, use_global_device_ids=true, to_apply=%region_17.18 | all-reduce | flops 9216 | bytes 55296 | tf_op jit(solution)/shard_map/psum | solution.py:315
  387.1 13.2 %all-gather.1 = bf16[4,4,2304]{2,1,0:T(4,128)(2,1)S(1)} all-gather(bf16[1,4,2304]{2,1,0:T(4,128)(2,1)S(1)} %bitcast.284), channel_id=2, replica_groups=mesh['narrow'=4,'wide'=8] {'narrow'}, dimensions={0}, use_global_device_ids=true | all-gather | bytes 92160 | tf_op jit(solution)/shard_map/all_gather | solution.py:320
  400.4 3.4 convolution_bitcast_fusion
  403.8 5.2 %copy.112 = f32[1,384,2304]{2,1,0:T(8,128)} copy(f32[1,384,2304]{1,2,0:T(8,128)} %convolution_bitcast_fusion) | data formatting | bytes 7077888
  411.1 70.6 %all-reduce.4.cloned.1.call-done = (f32[1,384,1152]{2,1,0:T(8,128)}, f32[1,384,384]{2,1,0:T(8,128)}, f32[1,384,1536]{2,1,0:T(8,128)}, f32[1,1536,384]{2,1,0:T(8,128)}) async-done(((f32[1,384,1152]{2,1,0:T(8,128)}, f32[1,384,384]{2,1,0:T(8,128)}, f32[1,384,1536]{2,1,0:T(8,128)}, f32[1,1536,384]{2,1,0:T(8,128)}), (f32[1,384,1152]{2,1,0:T(8,128)}, f32[1,384,384]{2,1,0:T(8,128)}, f32[1,384,1536]{2,1,0:T(8,128)}, ...) | async-done | bytes 7077904 | tf_op jit(solution)/shard_map/psum | solution.py:316
  481.7 2.9 copy.138
  485.5 1.4 copy.140
  486.9 1.4 copy.141
  (140 shorter events, 15.2 us)
Async XLA Ops:
  7.2 2.5 copy-start
  7.2 69.7 %all-gather.9.cloned.1.call-start = ((), (), s32[]{:S(2)}) async-start(), calls=%async_computation.1 | async-start | bytes 3538944 | tf_op jit(solution)/shard_map/all_gather | solution.py:96
  13.0 4.8 copy-start.29
  13.0 6.6 %copy-start.34 = (bf16[1,384]{1,0:T(2,128)(2,1)S(1)}, bf16[1,384]{1,0:T(2,128)(2,1)}, u32[]{:S(2)}) copy-start(bf16[1,384]{1,0:T(2,128)(2,1)} %param.21) | copy-start | bytes 2308
  13.0 6.6 %copy-start.25 = (bf16[1,1536]{1,0:T(2,128)(2,1)S(1)}, bf16[1,1536]{1,0:T(2,128)(2,1)}, u32[]{:S(2)}) copy-start(bf16[1,1536]{1,0:T(2,128)(2,1)} %param.23) | copy-start | bytes 9220
  13.0 6.7 %copy-start.40 = (s32[4]{0:T(128)S(1)}, s32[4]{0:T(128)}, u32[]{:S(2)}) copy-start(s32[4]{0:T(128)} %param.27) | copy-start | bytes 52
  13.0 7.9 %copy-start.35 = (bf16[1,384]{1,0:T(2,128)(2,1)S(1)}, bf16[1,384]{1,0:T(2,128)(2,1)}, u32[]{:S(2)}) copy-start(bf16[1,384]{1,0:T(2,128)(2,1)} %param.25) | copy-start | bytes 2308
  16.3 121.9 %all-gather.7.cloned.1.call-start = ((), (), s32[]{:S(2)}) async-start(), calls=%async_computation | async-start | bytes 3538944 | tf_op jit(solution)/shard_map/all_gather | solution.py:97
  17.1 183.1 %all-gather.11.cloned.1.call-start = ((), (), s32[]{:S(2)}) async-start(), calls=%async_computation.2 | async-start | bytes 3538944 | tf_op jit(solution)/shard_map/all_gather | solution.py:156
  17.8 252.0 %all-gather.13.cloned.1.call-start = ((), (), s32[]{:S(2)}) async-start(), calls=%async_computation.3 | async-start | bytes 3538944 | tf_op jit(solution)/shard_map/all_gather | solution.py:157
  20.9 143.1 %copy-start.36 = (f32[4]{0:T(128)}, f32[4]{0:T(128)S(1)}, u32[]{:S(2)}) copy-start(f32[4]{0:T(128)S(1)} %compare_convert_fusion) | copy-start | bytes 52
  146.9 5.4 %copy-start.1 = (f32[4,6,1024,128]{3,2,1,0:T(8,128)}, f32[4,6,1024,128]{3,2,1,0:T(8,128)S(1)}, u32[]{:S(2)}) copy-start(f32[4,6,1024,128]{3,2,1,0:T(8,128)S(1)} %get-tuple-element.98) | copy-start | bytes 37748740
  146.9 5.4 %copy-start.8 = (bf16[4,1024,384]{1,2,0:T(8,128)(2,1)S(1)}, bf16[4,1024,384]{1,2,0:T(8,128)(2,1)}, u32[]{:S(2)}) copy-start(bf16[4,1024,384]{1,2,0:T(8,128)(2,1)} %copy.91) | copy-start | bytes 9437188
  152.3 3.5 copy-start.3
  154.8 4.8 copy-start.6
  155.7 2.7 copy-start.37
  158.4 1.2 copy-start.20
  158.5 1.4 copy-start.38
  159.6 4.4 copy-start.4
  162.4 4.7 copy-start.12
  164.1 3.0 copy-start.14
  164.1 3.0 copy-start.17
  167.1 1.4 copy-start.15
  167.1 3.5 copy-start.5
  168.6 313.1 %all-reduce.4.cloned.1.call-start = ((), (), s32[]{:S(2)}) async-start(), calls=%async_computation.4 | async-start | bytes 14155776 | tf_op jit(solution)/shard_map/psum | solution.py:316
  189.9 64.9 %copy-start.7 = (bf16[4,128,6,64]{1,3,2,0:T(8,128)(2,1)S(1)}, bf16[4,128,6,64]{1,3,2,0:T(8,128)(2,1)}, u32[]{:S(2)}) copy-start(bf16[4,128,6,64]{1,3,2,0:T(8,128)(2,1)} %copy-done.6) | copy-start | bytes 1179652
  257.0 4.1 copy-start.13
  261.1 2.3 copy-start.2
  261.1 2.3 copy-start.16
  274.5 8.0 %copy-start.22 = (bf16[4,128,384]{1,2,0:T(8,128)(2,1)S(1)}, bf16[4,128,384]{1,2,0:T(8,128)(2,1)}, u32[]{:S(2)}) copy-start(bf16[4,128,384]{1,2,0:T(8,128)(2,1)} %copy.102) | copy-start | bytes 1179652
  282.5 14.6 %copy-start.21 = (bf16[4,128,384]{2,1,0:T(8,128)(2,1)S(1)}, bf16[4,128,384]{2,1,0:T(8,128)(2,1)}, u32[]{:S(2)}) copy-start(bf16[4,128,384]{2,1,0:T(8,128)(2,1)} %copy.106) | copy-start | bytes 1179652
  282.5 14.6 %copy-start.30 = (f32[4,384]{1,0:T(4,128)S(1)}, f32[4,384]{1,0:T(4,128)}, u32[]{:S(2)}) copy-start(f32[4,384]{1,0:T(4,128)} %copy-done.29) | copy-start | bytes 18436
  300.1 0.7 copy-start.31
  300.1 0.8 copy-start.39
  300.1 1.0 copy-start.33
  300.1 1.0 copy-start.32
  300.1 1.0 copy-start.24
  300.2 1.0 copy-start.28
  300.2 1.0 copy-start.27
  300.2 1.0 copy-start.26
  300.2 57.6 %copy-start.23 = (bf16[4,128,384]{2,1,0:T(8,128)(2,1)S(1)}, bf16[4,128,384]{2,1,0:T(8,128)(2,1)}, u32[]{:S(2)}) copy-start(bf16[4,128,384]{2,1,0:T(8,128)(2,1)} %copy.108) | copy-start | bytes 1179652
  357.8 2.4 copy-start.9
  357.8 2.4 copy-start.18
  481.7 3.0 copy-start.19
  481.7 3.8 copy-start.11
  484.6 2.2 copy-start.10
Sparse Core Ops, SparseCore 0:
  16.4 60.3 all-gather.8
  79.1 59.1 all-gather.6
  141.0 59.1 all-gather.10
  202.2 61.3 all-gather.12
  300.3 181.2 all-reduce.3
where the time goes:
time: 500 us; the launch traced here: 495 us
  waiting for transfers between devices  195 us (39%)
  blocking collectives  145 us (29%)
  matrix products  80.2 us (16%)
  local copies, waits for them, and re-layouts  50.5 us (10%)
  between operations  14.7 us (3%)
  other arithmetic  8.93 us (2%)
    psum x1, waiting for transfers between devices, body(): lax.psum((grad_qkv_w, grad_out_w, grad_out_b, grad_up_w, grad_up_b, grad_...  70.6 us
    all_gather x1, waiting for transfers between devices, attention_forward(): lax.all_gather(values_here, 'wide', axis=1, tiled=True)  56.7 us
    psum x1, blocking collectives, body(): lax.psum((grad_qkv_w, grad_out_w, grad_out_b, grad_up_w, grad_up_b, grad_...  56.6 us
    all_gather x1, waiting for transfers between devices, attention_forward(): lax.all_gather(keys_here, 'wide', axis=1, tiled=True)  55.9 us
    all_gather x1, blocking collectives, attention_backward(): lax.all_gather(delta, 'wide', axis=1, tiled=True)  27.3 us
    psum x1, blocking collectives, body(): grad_mods[layer] = lax.psum(local_mods, 'wide')  25.5 us
    all_gather x1, blocking collectives, attention_backward(): lax.all_gather(log_total, 'wide', axis=1, tiled=True)  22.7 us
    unnamed x92, local copies, waits for them, and re-layouts  16.1 us
  transfers between devices with their start and end apart: 5, of which 4 were waited for; matrix products, arithmetic and copies ran while one was open for 18% of the time, Pallas kernels for 0%

commit v1 on v0

--- a/solution.py
+++ b/solution.py
@@ -1,12 +1,766 @@
+import functools
+from types import SimpleNamespace
+
 import jax
 import jax.numpy as jnp
 from jax import lax
+from jax.experimental import pallas as pl
+from jax.experimental.pallas import tpu as pltpu
 from jax.sharding import PartitionSpec as P
 
+MESH = pl.DeviceIdType.MESH
+f32, bf16 = jnp.float32, jnp.bfloat16
+EPS = 1e-06
+ROOT_HALF = 0.7071067811865476
+INV_ROOT_2PI = 0.3989422804014327
+HEAD_DIM = 64
+
+
+def dot_nn(a, b):
+    return lax.dot_general(a, b, (((1,), (0,)), ((), ())), preferred_element_type=f32)
+
+
+def dot_nt(a, b):
+    return lax.dot_general(a, b, (((1,), (1,)), ((), ())), preferred_element_type=f32)
+
+
+def dot_tn(a, b):
+    return lax.dot_general(a, b, (((0,), (0,)), ((), ())), preferred_element_type=f32)
+
+
+def norm_rows(x):
+    centred = x - jnp.mean(x, axis=-1, keepdims=True)
+    inverse = lax.rsqrt(jnp.mean(centred * centred, axis=-1, keepdims=True) + EPS)
+    return centred * inverse, inverse
+
+
+def norm_rows_back(x, n, inverse):
+    first = jnp.mean(x, axis=-1, keepdims=True)
+    second = jnp.mean(x * n, axis=-1, keepdims=True)
+    return inverse * (x - first - n * second)
+
+
+def col_sum(x):
+    return jnp.sum(x, axis=0, keepdims=True)
+
+
+class Place:
+    def __init__(self):
+        narrow, wide = lax.axis_index("narrow"), lax.axis_index("wide")
+        self.y, self.c = narrow // 2, narrow % 2
+        self.z, self.x = wide // 2, wide % 2
+        self.wide = wide
+        self.low = wide % 4
+        self.half = wide // 4
+        self.rows_half = 1 - self.c
+        self.plane = 2 * self.y + self.x
+
+    def low_xor(self, i):
+        a = self.low
+        if i & 1:
+            a = a + 1 - 2 * (a % 2)
+        if i & 2:
+            a = a + 2 - 4 * (a // 2)
+        return a
+
+    def home(self, i):
+        slot = self.low_xor(i)
+        return slot, (2 * self.y + 1 - self.half, 4 * self.c + slot)
+
+    def source(self, i):
+        strip = self.low_xor(i)
+        return strip, (2 * self.y + self.half, 4 * self.rows_half + strip)
+
+    def core(self):
+        return (2 * self.y + 1 - self.c, self.wide)
+
+    def in_plane(self, k):
+        x = 1 - self.x if k & 1 else self.x
+        y = 1 - self.y if k & 2 else self.y
+        return 2 * y + x, (2 * y + self.c, 2 * self.z + x)
+
+    def along_z(self, k):
+        z = self.z
+        if k & 1:
+            z = z + 1 - 2 * (z % 2)
+        if k & 2:
+            z = z + 2 - 4 * (z // 2)
+        return z, (2 * self.y + self.c, 2 * z + self.x)
+
+
+class Wire:
+    def __init__(self, send_sems, recv_sems):
+        self.send_sems, self.recv_sems = send_sems, recv_sems
+        self.count = 0
+        self.sent = []
+
+    def copy(self, src, dst, device):
+        index = self.count
+        self.count += 1
+        made = pltpu.make_async_remote_copy(
+            src_ref=src,
+            dst_ref=dst,
+            send_sem=self.send_sems.at[index],
+            recv_sem=self.recv_sems.at[index],
+            device_id=device,
+            device_id_type=MESH,
+        )
+        made.start()
+        self.sent.append(made)
+        return made
+
+    def finish(self):
+        for made in self.sent:
+            made.wait_send()
+
+
+def main_kernel(sizes, names, *refs):
+    r = SimpleNamespace(**dict(zip(names, refs, strict=True)))
+    R, D, FF = sizes
+    M, N = 4 * R, 8 * R
+    MB = M // 2
+    pairs = D // 128
+    here = Place()
+    wire = Wire(r.send_sems, r.recv_sems)
+    local_sems = r.local_sems
+    local_count = [0]
+
+    def local(src, dst):
+        made = pltpu.make_async_copy(src, dst, local_sems.at[local_count[0]])
+        local_count[0] += 1
+        made.start()
+        return made
+
+    load_ada = local(r.ada_weight.at[0], r.ada_weight_v)
+    load_qkv = local(r.qkv_weight.at[0], r.qkv_weight_v)
+    load_rest = [
+        local(r.out_weight.at[0], r.out_weight_v),
+        local(r.up_weight.at[0], r.up_weight_v),
+        local(r.down_weight.at[0], r.down_weight_v),
+    ]
+
+    barrier = pltpu.get_barrier_semaphore()
+    partners = [here.core()]
+    partners += [here.home(i)[1] for i in range(4)] + [here.source(i)[1] for i in range(4)]
+    partners += [here.in_plane(k)[1] for k in (1, 2, 3)] + [here.along_z(k)[1] for k in (1, 2, 3)]
+    for device in partners:
+        pl.semaphore_signal(barrier, inc=1, device_id=device, device_id_type=MESH)
+    pl.semaphore_wait(barrier, len(partners))
+
+    def send_home(whole, landing):
+        place = pl.ds(pl.multiple_of(here.low * R, R), R)
+        made = []
+        for i in range(4):
+            slot, device = here.home(i)
+            made.append(wire.copy(whole.at[0, slot], landing.at[place, :], device))
+        return made
+
+    tokens_in = send_home(r.tokens, r.tokens_v)
+    cotangent_in = send_home(r.cotangent, r.cotangent_v)
+
+    group, slot = 2 * here.y + here.half, here.low
+    item_class = r.lead_class[group, slot]
+    live = (slot < r.group_count[group]).astype(f32)
+    table = r.emb_table[...].astype(f32)
+    class_col = lax.broadcasted_iota(jnp.int32, (table.shape[0], 1), 0)
+    onehot = (class_col == item_class).astype(f32)
+    embed = jnp.sum(onehot * table, axis=0, keepdims=True)
+    silu = embed * (1.0 / (1.0 + jnp.exp(-embed)))
+    high = silu.astype(bf16).astype(f32)
+    middle_part = (silu - high).astype(bf16).astype(f32)
+    low_part = silu - high - middle_part
+    row = lax.broadcasted_iota(jnp.int32, (16, D), 0)
+    parts = jnp.where(row == 0, high, jnp.where(row == 1, middle_part, jnp.where(row == 2, low_part, 0.0)))
+    load_ada.wait()
+    mods = r.mods
+    for k in range(6):
+        cols = pl.ds(k * D, D)
+        mods[k : k + 1, :] = col_sum(
+            dot_nn(parts.astype(bf16), r.ada_weight_v[:, cols])
+        ) + r.ada_bias[:, cols].astype(f32)
+
+    def mod(k):
+        return mods[k : k + 1, :]
+
+    acc = r.acc
+    acc[...] = jnp.zeros_like(acc)
+
+    load_qkv.wait()
+    lane = lax.broadcasted_iota(jnp.int32, (R, 128), 1)
+    left = lane < HEAD_DIM
+    kv, qst = r.kv, r.qst
+    kv_copies = []
+    own = pl.multiple_of(here.rows_half * M, M)
+    for i in range(4):
+        strip, _ = here.source(i)
+        tokens_in[i].wait_recv()
+        at = pl.multiple_of(strip * R, R)
+        rows = pl.ds(at, R)
+        normed, inverse = norm_rows(r.tokens_v[rows, :].astype(f32))
+        r.normed[rows, :] = normed
+        r.inverse[rows, :] = inverse
+        modulated = (normed * (1.0 + mod(1)) + mod(0)).astype(bf16)
+        r.modulated[rows, :] = modulated
+        projected = dot_nn(modulated, r.qkv_weight_v[...])
+        kv_rows = pl.ds(pl.multiple_of(own + at, R), R)
+        kv[kv_rows, :] = projected[:, D:].astype(bf16)
+        kv_copies.append(wire.copy(kv.at[kv_rows, :], kv.at[kv_rows, :], here.core()))
+        for p in range(pairs):
+            q = projected[:, p * 128 : (p + 1) * 128].astype(bf16) * HEAD_DIM ** (-0.5)
+            zero = jnp.zeros_like(q)
+            qst[p, pl.ds(at, R), :] = jnp.where(left, q, zero)
+            qst[p, pl.ds(pl.multiple_of(M + at, R), R), :] = jnp.where(left, zero, q)
+    for made in kv_copies:
+        made.wait_recv()
+
+    kvt, es, ots = r.kvt, r.es, r.ots
+    for b in range(2 * pairs):
+        kvt[b * 128 : (b + 1) * 128, :] = kv[:, b * 128 : (b + 1) * 128].T
+    QB = M // 2
+
+    def forward_block(j, carry):
+        p, qb = j // 4, j % 4
+        cols = pl.ds(pl.multiple_of(p * 128, 128), 128)
+        queries = pl.ds(pl.multiple_of(qb * QB, QB), QB)
+        scores = dot_nt(kv[:, cols], qst[p, queries, :])
+        top = jnp.max(scores, axis=0, keepdims=True)
+        raised = jnp.exp(scores - top)
+        inv = 1.0 / col_sum(raised)
+        raised = raised.astype(bf16)
+        es[p, :, queries] = raised
+        r.inv_sum[j] = inv
+        head = pl.multiple_of(p * 128 + (qb // 2) * HEAD_DIM, HEAD_DIM)
+        mixed = dot_nn(kvt[pl.ds(pl.multiple_of(D + head, HEAD_DIM), HEAD_DIM), :], raised) * inv
+        ots[pl.ds(head, HEAD_DIM), pl.ds(pl.multiple_of((qb % 2) * QB, QB), QB)] = mixed
+        return carry
+
+    lax.fori_loop(0, 4 * pairs, forward_block, 0)
+    att = r.att
+    for p in range(pairs):
+        att[:, p * 128 : (p + 1) * 128] = ots[p * 128 : (p + 1) * 128, :].T.astype(bf16)
+
+    for made in load_rest:
+        made.wait()
+    for made in cotangent_in:
+        made.wait_recv()
+    outw, upw, downw = r.out_weight_v, r.up_weight_v, r.down_weight_v
+    chunks = FF // D
+
+    def feed_block(t, carry):
+        rows = pl.ds(pl.multiple_of(t * MB, MB), MB)
+        branch = dot_nn(att[rows, :], outw[...]) + r.out_bias[...].astype(f32)
+        middle = r.tokens_v[rows, :].astype(f32) + mod(2) * branch
+        n, inverse = norm_rows(middle)
+        modulated = (n * (1.0 + mod(4)) + mod(3)).astype(bf16)
+        r.modulated_m[rows, :] = modulated
+
+        def up_chunk(ck, inner):
+            cols = pl.ds(pl.multiple_of(ck * D, D), D)
+            u = dot_nn(modulated, upw[:, cols]) + r.up_bias[:, cols].astype(f32)
+            phi = 0.5 * (1.0 + lax.erf(u * ROOT_HALF))
+            r.activated[rows, cols] = (u * phi).astype(bf16)
+            r.slope[:, cols] = phi + u * (INV_ROOT_2PI * jnp.exp(-0.5 * u * u))
+            return inner
+
+        lax.fori_loop(0, chunks, up_chunk, 0)
+        feed = dot_nn(r.activated[rows, :], downw[...]) + r.down_bias[...].astype(f32)
+        r.out_stage[rows, :] = ((middle + mod(5) * feed) * live).astype(bf16)
+        grad = r.cotangent_v[rows, :].astype(f32) * live
+        grad_feed = (grad * mod(5)).astype(bf16)
+        r.grad_feed[rows, :] = grad_feed
+        acc[5:6, :] += col_sum(grad * feed)
+        acc[8:9, :] += col_sum(grad_feed.astype(f32))
+
+        def down_chunk(ck, inner):
+            cols = pl.ds(pl.multiple_of(ck * D, D), D)
+            grad_up = (dot_nt(grad_feed, downw[cols, :]) * r.slope[:, cols]).astype(bf16)
+            r.grad_up[rows, cols] = grad_up
+            acc[pl.ds(9 + ck, 1), :] += col_sum(grad_up.astype(f32))
+            return inner
+
+        lax.fori_loop(0, chunks, down_chunk, 0)
+        back = dot_nt(r.grad_up[rows, :], upw[...])
+        acc[3:4, :] += col_sum(back)
+        acc[4:5, :] += col_sum(back * n)
+        grad_middle = grad + norm_rows_back(back * (1.0 + mod(4)), n, inverse)
+        r.grad_middle[rows, :] = grad_middle
+        acc[2:3, :] += col_sum(grad_middle * branch)
+        grad_branch = (grad_middle * mod(2)).astype(bf16)
+        r.grad_branch[rows, :] = grad_branch
+        acc[13:14, :] += col_sum(grad_branch.astype(f32))
+        r.grad_att[rows, :] = dot_nt(grad_branch, outw[...]).astype(bf16)
+        return carry
+
+    lax.fori_loop(0, 2, feed_block, 0)
+
+    def send_back(stage, landing):
+        made = []
+        for i in range(4):
+            strip, device = here.source(i)
+            rows = pl.ds(pl.multiple_of(strip * R, R), R)
+            made.append(wire.copy(stage.at[rows, :], landing.at[here.low], device))
+        return made
+
+    out_copies = send_back(r.out_stage, r.out_o)
+
+    part, total = r.part, r.total
+    piece_rows = 4 * D
+    core_rows, plane_rows, z_rows = piece_rows // 2, piece_rows // 8, piece_rows // 32
+    by_core, by_plane, by_z, by_z_back, by_plane_back, by_core_back = {}, {}, {}, {}, {}, {}
+
+    def piece_core(i):
+        base = i * piece_rows
+        src = part.at[pl.ds(pl.multiple_of(base + core_rows * (1 - here.c), core_rows), core_rows), :]
+        by_core[i] = [wire.copy(src, r.land_core.at[i], here.core())]
+
+    def own_core(i):
+        return pl.multiple_of(i * piece_rows + core_rows * here.c, core_rows)
+
+    def piece_plane(i):
+        for made in by_core[i]:
+            made.wait_recv()
+
+        def add(q, carry):
+            rows = pl.ds(pl.multiple_of(q * plane_rows, plane_rows), plane_rows)
+            mine = pl.ds(pl.multiple_of(own_core(i) + q * plane_rows, plane_rows), plane_rows)
+            r.sum_core[i, rows, :] = (
+                part[mine, :].astype(f32) + r.land_core[i, rows, :].astype(f32)
+            ).astype(bf16)
+            return carry
+
+        lax.fori_loop(0, 4, add, 0)
+        by_plane[i] = []
+        for k in (3, 1, 2):
+            q, device = here.in_plane(k)
+            rows = pl.ds(pl.multiple_of(q * plane_rows, plane_rows), plane_rows)
+            by_plane[i].append(
+                wire.copy(r.sum_core.at[i, rows, :], r.land_plane.at[i, k - 1], device)
+            )
+
+    def piece_z(i):
+        for made in by_plane[i]:
+            made.wait_recv()
+        rows = pl.ds(pl.multiple_of(here.plane * plane_rows, plane_rows), plane_rows)
+        summed = r.sum_core[i, rows, :].astype(f32)
+        for k in range(3):
+            summed = summed + r.land_plane[i, k].astype(f32)
+        r.sum_plane[i] = summed.astype(bf16)
+        by_z[i] = []
+        for k in (3, 2, 1):
+            z, device = here.along_z(k)
+            rows = pl.ds(pl.multiple_of(z * z_rows, z_rows), z_rows)
+            by_z[i].append(
+                wire.copy(r.sum_plane.at[i, rows, :], r.land_z.at[i, k - 1], device)
+            )
+
+    def own_plane(i):
+        return pl.multiple_of(own_core(i) + here.plane * plane_rows, plane_rows)
+
+    def piece_z_back(i):
+        for made in by_z[i]:
+            made.wait_recv()
+        rows = pl.ds(pl.multiple_of(here.z * z_rows, z_rows), z_rows)
+        summed = r.sum_plane[i, rows, :].astype(f32)
+        for k in range(3):
+            summed = summed + r.land_z[i, k].astype(f32)
+        mine = pl.ds(pl.multiple_of(own_plane(i) + here.z * z_rows, z_rows), z_rows)
+        total[mine, :] = summed.astype(bf16)
+        by_z_back[i] = [
+            wire.copy(total.at[mine, :], total.at[mine, :], here.along_z(k)[1]) for k in (3, 2, 1)
+        ]
+
+    def piece_plane_back(i):
+        for made in by_z_back[i]:
+            made.wait_recv()
+        mine = pl.ds(own_plane(i), plane_rows)
+        by_plane_back[i] = [
+            wire.copy(total.at[mine, :], total.at[mine, :], here.in_plane(k)[1]) for k in (3, 1, 2)
+        ]
+
+    def piece_core_back(i):
+        for made in by_plane_back[i]:
+            made.wait_recv()
+        mine = pl.ds(own_core(i), core_rows)
+        by_core_back[i] = [wire.copy(total.at[mine, :], total.at[mine, :], here.core())]
+
+    stored = []
+
+    def piece_store(i):
+        for made in by_core_back[i]:
+            made.wait_recv()
+        rows = pl.ds(i * piece_rows, piece_rows)
+        stored.append(local(total.at[rows, :], r.grads_o.at[rows, :]))
+
+    def down_grad(ck, carry):
+        cols = pl.ds(pl.multiple_of(ck * D, D), D)
+        part[cols, :] = dot_tn(r.activated[:, cols], r.grad_feed[...]).astype(bf16)
+        return carry
+
+    lax.fori_loop(0, chunks, down_grad, 0)
+    piece_core(0)
+
+    def up_grad(ck, carry):
+        cols = pl.ds(pl.multiple_of(ck * D, D), D)
+        rows = pl.ds(pl.multiple_of(FF + ck * D, D), D)
+        part[rows, :] = dot_tn(r.modulated_m[...], r.grad_up[:, cols]).astype(bf16)
+        return carry
+
+    lax.fori_loop(0, chunks, up_grad, 0)
+    piece_core(1)
+    piece_plane(0)
+    part[2 * FF : 2 * FF + D, :] = dot_tn(att[...], r.grad_branch[...]).astype(bf16)
+
+    gat, qgt = r.gat, r.qgt
+    for p in range(pairs):
+        gat[p * 128 : (p + 1) * 128, :] = r.grad_att[:, p * 128 : (p + 1) * 128].T.astype(f32)
+    zero_half = jnp.zeros((HEAD_DIM, QB), bf16)
+    gst, gstt, deltas, dss = r.gst, r.gstt, r.deltas, r.dss
+    dkv = r.dkv
+    dkv_copies = []
+    other = pl.multiple_of((1 - here.rows_half) * M, M)
+    for p in range(pairs):
+        for qb in range(4):
+            half = qb // 2
+            head = p * 128 + half * HEAD_DIM
+            queries = slice((qb % 2) * QB, (qb % 2) * QB + QB)
+            inv = r.inv_sum[4 * p + qb]
+            scaled = gat[head : head + HEAD_DIM, queries] * inv
+            deltas[qb] = col_sum(scaled * ots[head : head + HEAD_DIM, queries])
+            scaled = scaled.astype(bf16)
+            filled = [scaled, zero_half] if half == 0 else [zero_half, scaled]
+            gstt[:, qb * QB : (qb + 1) * QB] = jnp.concatenate(filled, axis=0)
+        gst[...] = gstt[...].T
+
+        def backward_block(qb, carry, p=p):
+            queries = pl.ds(pl.multiple_of(qb * QB, QB), QB)
+            slope = dot_nn(kv[:, D + p * 128 : D + (p + 1) * 128], gstt[:, queries])
+            grad_scores = (es[p, :, queries].astype(f32) * (slope - deltas[qb])).astype(bf16)
+            dss[:, queries] = grad_scores
+            head = pl.multiple_of(p * 128 + (qb // 2) * HEAD_DIM, HEAD_DIM)
+            grad_q = dot_nn(kvt[pl.ds(head, HEAD_DIM), :], grad_scores) * HEAD_DIM ** (-0.5)
+            qgt[pl.ds(head, HEAD_DIM), pl.ds(pl.multiple_of((qb % 2) * QB, QB), QB)] = grad_q
+            return carry
+
+        lax.fori_loop(0, 4, backward_block, 0)
+        dkv[p, :, 0:128] = dot_nn(dss[...], qst[p]).astype(bf16)
+        dkv[p, :, 128:256] = dot_nn(es[p], gst[...]).astype(bf16)
+        dkv_copies.append(wire.copy(dkv.at[p, pl.ds(other, M), :], r.land_dkv.at[p], here.core()))
+        if p == 0:
+            piece_plane(1)
+            piece_z(0)
+        if p == 1:
+            piece_z(1)
+            piece_z_back(0)
+    gp = r.grad_projected
+    for p in range(pairs):
+        cols = slice(p * 128, (p + 1) * 128)
+        gp[:, cols] = qgt[cols, :].T.astype(bf16)
+        dkv_copies[p].wait_recv()
+        summed = dkv[p, pl.ds(own, M), :].astype(f32) + r.land_dkv[p].astype(f32)
+        gp[:, D + p * 128 : D + (p + 1) * 128] = summed[:, :128].astype(bf16)
+        gp[:, 2 * D + p * 128 : 2 * D + (p + 1) * 128] = summed[:, 128:].astype(bf16)
+
+    for b in range(3):
+        cols = slice(b * D, (b + 1) * D)
+        rows = slice(2 * FF + (b + 1) * D, 2 * FF + (b + 2) * D)
+        part[rows, :] = dot_tn(r.modulated[...], gp[:, cols]).astype(bf16)
+    piece_core(2)
+
+    def token_block(t, carry):
+        rows = pl.ds(pl.multiple_of(t * MB, MB), MB)
+        back = dot_nt(gp[rows, :], r.qkv_weight_v[...])
+        n = r.normed[rows, :]
+        acc[0:1, :] += col_sum(back)
+        acc[1:2, :] += col_sum(back * n)
+        grad = r.grad_middle[rows, :] + norm_rows_back(
+            back * (1.0 + mod(1)), n, r.inverse[rows, :]
+        )
+        r.gtok_stage[rows, :] = grad.astype(bf16)
+        return carry
+
+    lax.fori_loop(0, 2, token_block, 0)
+    piece_plane(2)
+    gtok_copies = send_back(r.gtok_stage, r.gtok_o)
+
+    small = r.small
+    for k in range(6):
+        small[4 * k : 4 * k + 4, :] = onehot * acc[k : k + 1, :]
+    small[24:32, :] = acc[8:16, :]
+    rows_here = pl.ds(pl.multiple_of(16 * here.c, 16), 16)
+    rows_there = pl.ds(pl.multiple_of(16 * (1 - here.c), 16), 16)
+    flight = wire.copy(small.at[rows_there, :], r.land_small.at[0], here.core())
+    flight.wait_recv()
+    r.small_a[...] = small[rows_here, :] + r.land_small[0]
+    flight = [
+        wire.copy(r.small_a, r.land_small.at[k], here.in_plane(k)[1]) for k in (3, 1, 2)
+    ]
+    piece_z_back(1)
+    for made in flight:
+        made.wait_recv()
+    r.small_b[...] = (
+        r.small_a[...] + r.land_small[1] + r.land_small[2] + r.land_small[3]
+    )
+    flight = [
+        wire.copy(r.small_b, r.land_small.at[3 + k], here.along_z(k)[1]) for k in (3, 2, 1)
+    ]
+    piece_plane_back(0)
+    piece_z(2)
+    piece_plane_back(1)
+    for made in flight:
+        made.wait_recv()
+    small_sum = r.small_sum
+    small_sum[rows_here, :] = (
+        r.small_b[...] + r.land_small[4] + r.land_small[5] + r.land_small[6]
+    )
+    flight = wire.copy(small_sum.at[rows_here, :], small_sum.at[rows_here, :], here.core())
+    piece_core_back(0)
+    piece_z_back(2)
+    piece_core_back(1)
+    flight.wait_recv()
+    stored.append(local(small_sum, r.small_o))
+    piece_store(0)
+    piece_plane_back(2)
+    piece_store(1)
+    piece_core_back(2)
+    piece_store(2)
+    for made in out_copies + gtok_copies:
+        made.wait_recv()
+    wire.finish()
+    for made in stored:
+        made.wait()
+
+
+def last_kernel(sizes, names, *refs):
+    r = SimpleNamespace(**dict(zip(names, refs, strict=True)))
+    D, FF = sizes
+    sems = r.sems
+    count = [0]
+
+    def local(src, dst):
+        made = pltpu.make_async_copy(src, dst, sems.at[count[0]])
+        count[0] += 1
+        made.start()
+        return made
+
+    small_in = local(r.small_i, r.small_i_v)
+    ada_in = local(r.ada_weight, r.ada_weight_v)
+    out_in = local(r.out_i, r.out_i_v)
+    gtok_in = local(r.gtok_i, r.gtok_i_v)
+    grads_in = []
+    for b in range(3):
+        rows = pl.ds(b * 4 * D, 4 * D)
+        grads_in.append(local(r.grads_i.at[rows, :], r.grads_v.at[rows, :]))
+    outs = []
+    small_in.wait()
+    small = r.small_i_v
+    table = r.emb_table[...].astype(f32)
+    sigmoid = 1.0 / (1.0 + jnp.exp(-table))
+    silu = table * sigmoid
+
+    def split(v):
+        high = v.astype(bf16).astype(f32)
+        return high, v - high
+
+    silu_high, silu_low = split(silu)
+    zero = jnp.zeros_like(silu)
+    left = jnp.concatenate([silu_high, silu_low, silu_high, zero], axis=0).astype(bf16)
+    grad_silu = jnp.zeros_like(table)
+    ada_in.wait()
+    for k in range(6):
+        cols = slice(k * D, (k + 1) * D)
+        block = small[4 * k : 4 * k + 4, :]
+        high, low = split(block)
+        right = jnp.concatenate([high, high, low, zero], axis=0).astype(bf16)
+        r.gada_v[:, cols] = dot_tn(left, right)
+        r.gada_b[:, cols] = col_sum(block)
+        both = jnp.concatenate([high, low, zero, zero], axis=0).astype(bf16)
+        found = dot_nt(both, r.ada_weight_v[0, :, cols])
+        grad_silu = grad_silu + found[0:4, :] + found[4:8, :]
+    outs.append(local(r.gada_v, r.gada.at[0]))
+    r.table_o[...] = grad_silu * (sigmoid + table * sigmoid * (1.0 - sigmoid))
+    r.down_b[...] = small[24:25, :]
+    for k in range(FF // D):
+        r.up_b[:, k * D : (k + 1) * D] = small[25 + k : 26 + k, :]
+    r.out_b[...] = small[29:30, :]
+    for arrived, given, wide_v, result in (
+        (out_in, r.out_i_v, r.out_v, r.out),
+        (gtok_in, r.gtok_i_v, r.gtok_v, r.gtok),
+    ):
+        arrived.wait()
+        for s in range(4):
+            wide_v[s] = given[s].astype(f32)
+        outs.append(local(wide_v, result.at[0]))
+    grads = r.grads_v
+    grads_in[0].wait()
+    for k in range(FF // D):
+        r.gdown_v[k * D : (k + 1) * D, :] = grads[k * D : (k + 1) * D, :].astype(f32)
+    outs.append(local(r.gdown_v, r.gdown.at[0]))
+    grads_in[1].wait()
+    for k in range(FF // D):
+        r.gup_v[:, k * D : (k + 1) * D] = grads[FF + k * D : FF + (k + 1) * D, :].astype(f32)
+    outs.append(local(r.gup_v, r.gup.at[0]))
+    grads_in[2].wait()
+    r.gout_v[...] = grads[2 * FF : 2 * FF + D, :].astype(f32)
+    outs.append(local(r.gout_v, r.gout.at[0]))
+    for k in range(3):
+        rows = slice(2 * FF + (k + 1) * D, 2 * FF + (k + 2) * D)
+        r.gqkv_v[:, k * D : (k + 1) * D] = grads[rows, :].astype(f32)
+    outs.append(local(r.gqkv_v, r.gqkv.at[0]))
+    for made in outs:
+        made.wait()
+
+
+def fast_body(*args):
+    tokens, emb_table, ada_weight, up_weight = args[0], args[2], args[3], args[8]
+    R, D = tokens.shape[2:]
+    FF = up_weight.shape[2]
+    M, N = 4 * R, 8 * R
+    pairs = D // 128
+    total_rows = 2 * FF + 4 * D
+    vmem = pl.BlockSpec(memory_space=pltpu.VMEM)
+    smem = pl.BlockSpec(memory_space=pltpu.SMEM)
+    anywhere = pl.BlockSpec(memory_space=pl.ANY)
+    arguments = dict(
+        tokens=anywhere,
+        cotangent=anywhere,
+        emb_table=vmem,
+        ada_weight=anywhere,
+        ada_bias=vmem,
+        qkv_weight=anywhere,
+        out_weight=anywhere,
+        out_bias=vmem,
+        up_weight=anywhere,
+        up_bias=vmem,
+        down_weight=anywhere,
+        down_bias=vmem,
+        lead_class=smem,
+        group_count=smem,
+    )
+    piece = 4 * D
+    scratch = dict(
+        ada_weight_v=pltpu.VMEM((D, 6 * D), bf16),
+        qkv_weight_v=pltpu.VMEM((D, 3 * D), bf16),
+        out_weight_v=pltpu.VMEM((D, D), bf16),
+        up_weight_v=pltpu.VMEM((D, FF), bf16),
+        down_weight_v=pltpu.VMEM((FF, D), bf16),
+        tokens_v=pltpu.VMEM((M, D), bf16),
+        cotangent_v=pltpu.VMEM((M, D), bf16),
+        mods=pltpu.VMEM((8, D), f32),
+        acc=pltpu.VMEM((16, D), f32),
+        normed=pltpu.VMEM((M, D), f32),
+        inverse=pltpu.VMEM((M, 1), f32),
+        modulated=pltpu.VMEM((M, D), bf16),
+        kv=pltpu.VMEM((N, 2 * D), bf16),
+        kvt=pltpu.VMEM((2 * D, N), bf16),
+        qst=pltpu.VMEM((pairs, 2 * M, 128), bf16),
+        es=pltpu.VMEM((pairs, N, 2 * M), bf16),
+        inv_sum=pltpu.VMEM((4 * pairs, 1, M // 2), f32),
+        ots=pltpu.VMEM((D, M), f32),
+        att=pltpu.VMEM((M, D), bf16),
+        modulated_m=pltpu.VMEM((M, D), bf16),
+        activated=pltpu.VMEM((M, FF), bf16),
+        slope=pltpu.VMEM((M // 2, FF), f32),
+        out_stage=pltpu.VMEM((M, D), bf16),
+        grad_feed=pltpu.VMEM((M, D), bf16),
+        grad_up=pltpu.VMEM((M, FF), bf16),
+        grad_middle=pltpu.VMEM((M, D), f32),
+        grad_branch=pltpu.VMEM((M, D), bf16),
+        grad_att=pltpu.VMEM((M, D), bf16),
+        gat=pltpu.VMEM((D, M), f32),
+        qgt=pltpu.VMEM((D, M), f32),
+        gst=pltpu.VMEM((2 * M, 128), bf16),
+        gstt=pltpu.VMEM((128, 2 * M), bf16),
+        deltas=pltpu.VMEM((4, 1, M // 2), f32),
+        dss=pltpu.VMEM((N, 2 * M), bf16),
+        dkv=pltpu.VMEM((pairs, N, 256), bf16),
+        land_dkv=pltpu.VMEM((pairs, M, 256), bf16),
+        grad_projected=pltpu.VMEM((M, 3 * D), bf16),
+        gtok_stage=pltpu.VMEM((M, D), bf16),
+        part=pltpu.VMEM((total_rows, D), bf16),
+        total=pltpu.VMEM((total_rows, D), bf16),
+        land_core=pltpu.VMEM((3, piece // 2, D), bf16),
+        sum_core=pltpu.VMEM((3, piece // 2, D), bf16),
+        land_plane=pltpu.VMEM((3, 3, piece // 8, D), bf16),
+        sum_plane=pltpu.VMEM((3, piece // 8, D), bf16),
+        land_z=pltpu.VMEM((3, 3, piece // 32, D), bf16),
+        small=pltpu.VMEM((32, D), f32),
+        small_a=pltpu.VMEM((16, D), f32),
+        small_b=pltpu.VMEM((16, D), f32),
+        small_sum=pltpu.VMEM((32, D), f32),
+        land_small=pltpu.VMEM((7, 16, D), f32),
+        send_sems=pltpu.SemaphoreType.DMA((80,)),
+        recv_sems=pltpu.SemaphoreType.DMA((80,)),
+        local_sems=pltpu.SemaphoreType.DMA((12,)),
+    )
+    mids = dict(
+        out_o=jax.ShapeDtypeStruct((4, R, D), bf16),
+        gtok_o=jax.ShapeDtypeStruct((4, R, D), bf16),
+        grads_o=jax.ShapeDtypeStruct((total_rows, D), bf16),
+        small_o=jax.ShapeDtypeStruct((32, D), f32),
+    )
+    names = tuple(arguments) + tuple(mids) + tuple(scratch)
+    middle = pl.pallas_call(
+        functools.partial(main_kernel, (R, D, FF), names),
+        out_shape=tuple(mids.values()),
+        in_specs=list(arguments.values()),
+        out_specs=(anywhere,) * 4,
+        scratch_shapes=list(scratch.values()),
+        compiler_params=pltpu.CompilerParams(
+            collective_id=0, has_side_effects=True, vmem_limit_bytes=60 << 20
+        ),
+        name="block_forward_backward",
+    )(*args)
+    outs = dict(
+        out=((1, 4, R, D), anywhere),
+        gtok=((1, 4, R, D), anywhere),
+        table_o=((emb_table.shape[0], D), vmem),
+        gada=((1, D, 6 * D), anywhere),
+        gada_b=((1, 6 * D), vmem),
+        gqkv=((1, D, 3 * D), anywhere),
+        gout=((1, D, D), anywhere),
+        out_b=((1, D), vmem),
+        gup=((1, D, FF), anywhere),
+        up_b=((1, FF), vmem),
+        gdown=((1, FF, D), anywhere),
+        down_b=((1, D), vmem),
+    )
+    ins = dict(
+        out_i=anywhere,
+        gtok_i=anywhere,
+        grads_i=anywhere,
+        small_i=anywhere,
+        emb_table=vmem,
+        ada_weight=anywhere,
+    )
+    scratch = dict(
+        out_i_v=pltpu.VMEM((4, R, D), bf16),
+        gtok_i_v=pltpu.VMEM((4, R, D), bf16),
+        grads_v=pltpu.VMEM((total_rows, D), bf16),
+        small_i_v=pltpu.VMEM((32, D), f32),
+        ada_weight_v=pltpu.VMEM((1, D, 6 * D), bf16),
+        out_v=pltpu.VMEM((4, R, D), f32),
+        gtok_v=pltpu.VMEM((4, R, D), f32),
+        gada_v=pltpu.VMEM((D, 6 * D), f32),
+        gqkv_v=pltpu.VMEM((D, 3 * D), f32),
+        gout_v=pltpu.VMEM((D, D), f32),
+        gup_v=pltpu.VMEM((D, FF), f32),
+        gdown_v=pltpu.VMEM((FF, D), f32),
+        sems=pltpu.SemaphoreType.DMA((16,)),
+    )
+    names = tuple(ins) + tuple(outs) + tuple(scratch)
+    return pl.pallas_call(
+        functools.partial(last_kernel, (D, FF), names),
+        out_shape=tuple(jax.ShapeDtypeStruct(size, f32) for size, _ in outs.values()),
+        in_specs=list(ins.values()),
+        out_specs=tuple(space for _, space in outs.values()),
+        scratch_shapes=list(scratch.values()),
+        compiler_params=pltpu.CompilerParams(vmem_limit_bytes=60 << 20),
+        name="widen_and_embed",
+    )(*middle, emb_table, ada_weight)
+
+
 HEADS = 6
-HEAD_DIM = 64
 LAYERS = 1
-
 
 epsilon = 1e-06
 highest = lax.Precision.HIGHEST
@@ -380,4 +1134,5 @@
         P(),
         P(),
     )
-    return jax.shard_map(body, mesh=mesh, in_specs=in_specs, out_specs=out_specs, check_vma=False)
+    by_item = dict(mesh.shape) == {"narrow": 4, "wide": 8}
+    return jax.shard_map(fast_body if by_item else body, mesh=mesh, in_specs=in_specs, out_specs=out_specs, check_vma=False)

time: 500 us -> 118 us (0.24)
  waiting for transfers between devices: 195 us -> 0 us
  blocking collectives: 145 us -> 0 us
  Pallas kernels: 0 us -> 117 us
  matrix products: 80.2 us -> 0 us
  local copies, waits for them, and re-layouts: 50.5 us -> 0 us
  between operations: 14.7 us -> 0.82 us
  other arithmetic: 8.93 us -> 0 us
    all_gather x4 -> x0, waiting for transfers between devices: 123 us -> none  [the longest x1 56.7 us: attention_forward(): lax.all_gather(values_here, 'wide', axis=1, tiled=True)]
    pallas_call x0 -> x2, Pallas kernels: none -> 117 us  [the longest x1 108 us: fast_body(): pl.pallas_call(functools.partial(main_kernel, (R, D, FF), names), out_sha...]
    psum x2 -> x0, blocking collectives: 82.1 us -> none  [the longest x1 56.6 us: body(): lax.psum((grad_qkv_w, grad_out_w, grad_out_b, grad_up_w, grad_up_b, grad_...]
    dot_general x24 -> x0, matrix products: 80.2 us -> none  [the longest x1 12.5 us: attention_backward(): jnp.einsum('snhp,snhe->sphe', grad_scores, piece_queries, preferred_eleme...]
    psum x1 -> x0, waiting for transfers between devices: 70.6 us -> none  [body(): lax.psum((grad_qkv_w, grad_out_w, grad_out_b, grad_up_w, grad_up_b, grad_...]
    all_gather x3 -> x0, blocking collectives: 63.2 us -> none  [the longest x1 27.3 us: attention_backward(): lax.all_gather(delta, 'wide', axis=1, tiled=True)]
    all_gather x4 -> x0, local copies, waits for them, and re-layouts: 18.6 us -> none  [the longest x1 4.68 us: attention_forward(): lax.all_gather(keys_here, 'wide', axis=1, tiled=True)]
    unnamed x92 -> x0, local copies, waits for them, and re-layouts: 16.1 us -> none
  transfers between devices with their start and end apart: 5 -> 0, of which waited for: 4 -> 0; matrix products, arithmetic and copies ran while one was open for 18% -> 0% of each run, Pallas kernels for 0% -> 0%
where the time goes in v1:
time: 118 us
  Pallas kernels  117 us (99%)
    pallas_call x1, Pallas kernels, fast_body(): pl.pallas_call(functools.partial(main_kernel, (R, D, FF), names), out_sha...  108 us
    pallas_call x1, Pallas kernels, fast_body(): pl.pallas_call(functools.partial(last_kernel, (D, FF), names), out_shape=...  8.34 us

profile of v1, /device:TPU:9, one launch (start us, length us, event | category | flops | bytes accessed | tf_op | source)
XLA Modules:
  0.0 117.6 jit_solution(12603261108135415589)
XLA Ops:
  0.6 108.4 %block_forward_backward.1 = (bf16[4,128,384]{2,1,0:T(8,128)(2,1)}, bf16[4,128,384]{2,1,0:T(8,128)(2,1)}, bf16[4608,384]{1,0:T(8,128)(2,1)}, f32[32,384]{1,0:T(8,128)}) custom-call(bf16[1,4,128,384]{3,2,1,0:T(8,128)(2,1)} %refs_0_.1, bf16[1,4,128,384]{3,2,1,0:T(8,128)(2,1)} %refs_1_.1, bf16[4,384]{1,0:T(4,128)(2,1)} %refs_4_.3, ...), custom_call_target="tpu_custom_call" | custom-call | tf_op jit(solution)/shard_map/block_forward_backward/pallas_call | solution.py:702
  109.1 8.3 %widen_and_embed.1 = (f32[1,4,128,384]{3,2,1,0:T(8,128)}, f32[1,4,128,384]{3,2,1,0:T(8,128)}, f32[4,384]{1,0:T(4,128)}, f32[1,384,2304]{2,1,0:T(8,128)}, f32[1,2...) custom-call(bf16[4,128,384]{2,1,0:T(8,128)(2,1)} %get-tuple-element., ...), custom_call_target="tpu_custom_call" | custom-call | tf_op jit(solution)/shard_map/widen_and_embed/pallas_call | solution.py:751

commit v2 on v1

--- a/solution.py
+++ b/solution.py
@@ -14,6 +14,37 @@
 ROOT_HALF = 0.7071067811865476
 INV_ROOT_2PI = 0.3989422804014327
 HEAD_DIM = 64
+EARLY = 6
+FORMS = (False, False, False, False, False, False, False, False, False)
+PLAN = (
+    (),
+    (),
+    (),
+    (),
+    (),
+    (0, 1),
+    (2, 3),
+    (),
+    (4,),
+    (5,),
+    (),
+    (0,),
+    (),
+    (),
+    (1,),
+    (),
+    (),
+    (2, 0),
+    (),
+    (3, 6, 1),
+    (),
+    (4,),
+    (),
+    (2, 5),
+    (0, 7, 3, 6, 1, 4, 8),
+    (2,),
+    (5, 9, 3, 0, 6, 0, 4, 7, 1, 1, 8, 2, 2, 5, 6, 7, 9, 8, 3, 3, 4, 7, 4, 5, 9, 5, 8, 9, 6, 6, 7, 7, 8, 8),
+)
 
 
 def dot_nn(a, b):
@@ -53,7 +84,6 @@
         self.low = wide % 4
         self.half = wide // 4
         self.rows_half = 1 - self.c
-        self.plane = 2 * self.y + self.x
 
     def low_xor(self, i):
         a = self.low
@@ -109,6 +139,10 @@
         self.sent.append(made)
         return made
 
+    def sent_out(self, made):
+        made.wait_send()
+        self.sent.remove(made)
+
     def finish(self):
         for made in self.sent:
             made.wait_send()
@@ -132,7 +166,14 @@
         return made
 
     load_ada = local(r.ada_weight.at[0], r.ada_weight_v)
-    load_qkv = local(r.qkv_weight.at[0], r.qkv_weight_v)
+    load_qkv = [
+        local(
+            r.qkv_weight.at[0, :, pl.ds(b * D + p * 128, 128)],
+            r.qkv_weight_v.at[p, :, pl.ds(b * 128, 128)],
+        )
+        for p in range(pairs)
+        for b in range(3)
+    ]
     load_rest = [
         local(r.out_weight.at[0], r.out_weight_v),
         local(r.up_weight.at[0], r.up_weight_v),
@@ -156,7 +197,6 @@
         return made
 
     tokens_in = send_home(r.tokens, r.tokens_v)
-    cotangent_in = send_home(r.cotangent, r.cotangent_v)
 
     group, slot = 2 * here.y + here.half, here.low
     item_class = r.lead_class[group, slot]
@@ -185,7 +225,8 @@
     acc = r.acc
     acc[...] = jnp.zeros_like(acc)
 
-    load_qkv.wait()
+    for made in load_qkv:
+        made.wait()
     lane = lax.broadcasted_iota(jnp.int32, (R, 128), 1)
     left = lane < HEAD_DIM
     kv, qst = r.kv, r.qst
@@ -201,84 +242,105 @@
         r.inverse[rows, :] = inverse
         modulated = (normed * (1.0 + mod(1)) + mod(0)).astype(bf16)
         r.modulated[rows, :] = modulated
-        projected = dot_nn(modulated, r.qkv_weight_v[...])
         kv_rows = pl.ds(pl.multiple_of(own + at, R), R)
-        kv[kv_rows, :] = projected[:, D:].astype(bf16)
-        kv_copies.append(wire.copy(kv.at[kv_rows, :], kv.at[kv_rows, :], here.core()))
         for p in range(pairs):
-            q = projected[:, p * 128 : (p + 1) * 128].astype(bf16) * HEAD_DIM ** (-0.5)
+            projected = dot_nn(modulated, r.qkv_weight_v[p]).astype(bf16)
+            kv[p, kv_rows, :] = projected[:, 128:]
+            q = projected[:, :128] * HEAD_DIM ** (-0.5)
             zero = jnp.zeros_like(q)
             qst[p, pl.ds(at, R), :] = jnp.where(left, q, zero)
             qst[p, pl.ds(pl.multiple_of(M + at, R), R), :] = jnp.where(left, zero, q)
+        kv_copies.append(wire.copy(kv.at[:, kv_rows, :], kv.at[:, kv_rows, :], here.core()))
+    for made in tokens_in:
+        wire.sent_out(made)
+    cotangent_in = send_home(r.cotangent, r.cotangent_v)
     for made in kv_copies:
         made.wait_recv()
 
     kvt, es, ots = r.kvt, r.es, r.ots
-    for b in range(2 * pairs):
-        kvt[b * 128 : (b + 1) * 128, :] = kv[:, b * 128 : (b + 1) * 128].T
+    for p in range(pairs):
+        kvt[p] = kv[p].T
     QB = M // 2
-
-    def forward_block(j, carry):
+    CB = N // 4
+    scores = (r.scores_a, r.scores_b)
+
+    def score_rows(j, c):
         p, qb = j // 4, j % 4
-        cols = pl.ds(pl.multiple_of(p * 128, 128), 128)
-        queries = pl.ds(pl.multiple_of(qb * QB, QB), QB)
-        scores = dot_nt(kv[:, cols], qst[p, queries, :])
-        top = jnp.max(scores, axis=0, keepdims=True)
-        raised = jnp.exp(scores - top)
-        inv = 1.0 / col_sum(raised)
-        raised = raised.astype(bf16)
-        es[p, :, queries] = raised
-        r.inv_sum[j] = inv
-        head = pl.multiple_of(p * 128 + (qb // 2) * HEAD_DIM, HEAD_DIM)
-        mixed = dot_nn(kvt[pl.ds(pl.multiple_of(D + head, HEAD_DIM), HEAD_DIM), :], raised) * inv
-        ots[pl.ds(head, HEAD_DIM), pl.ds(pl.multiple_of((qb % 2) * QB, QB), QB)] = mixed
-        return carry
-
-    lax.fori_loop(0, 4 * pairs, forward_block, 0)
+        found = dot_nt(kv[p, c * CB : (c + 1) * CB, :128], qst[p, qb * QB : (qb + 1) * QB, :])
+        scores[j % 2][c * CB : (c + 1) * CB, :] = found
+        return jnp.max(found.reshape(CB // 8, 8, QB), axis=0)
+
+    def mix(j):
+        p, qb = j // 4, j % 4
+        half = qb // 2 * HEAD_DIM
+        mixed = dot_nn(kvt[p, 128 + half : 128 + half + HEAD_DIM, :], es[p, :, qb * QB : (qb + 1) * QB])
+        head = slice(p * 128 + half, p * 128 + half + HEAD_DIM)
+        ots[head, qb % 2 * QB : (qb % 2 + 1) * QB] = mixed * r.inv_sum[j]
+
+    tops = [score_rows(0, c) for c in range(4)]
+    for j in range(4 * pairs):
+        p, qb = j // 4, j % 4
+        top = jnp.maximum(jnp.maximum(tops[0], tops[1]), jnp.maximum(tops[2], tops[3]))
+        top = jnp.max(top, axis=0, keepdims=True)
+        tops, sums = [], []
+        for c in range(4):
+            keys = slice(c * CB, (c + 1) * CB)
+            if j + 1 < 4 * pairs:
+                tops.append(score_rows(j + 1, c))
+            raised = jnp.exp(scores[j % 2][keys, :] - top)
+            sums.append(jnp.sum(raised.reshape(CB // 8, 8, QB), axis=0))
+            es[p, keys, qb * QB : (qb + 1) * QB] = raised.astype(bf16)
+            if c == 0 and j > 0:
+                mix(j - 1)
+        r.inv_sum[j] = 1.0 / col_sum((sums[0] + sums[1]) + (sums[2] + sums[3]))
+    mix(4 * pairs - 1)
     att = r.att
     for p in range(pairs):
         att[:, p * 128 : (p + 1) * 128] = ots[p * 128 : (p + 1) * 128, :].T.astype(bf16)
 
     for made in load_rest:
         made.wait()
-    for made in cotangent_in:
-        made.wait_recv()
     outw, upw, downw = r.out_weight_v, r.up_weight_v, r.down_weight_v
     chunks = FF // D
 
-    def feed_block(t, carry):
-        rows = pl.ds(pl.multiple_of(t * MB, MB), MB)
+    def send_back(stage, landing):
+        made = []
+        for i in range(4):
+            strip, device = here.source(i)
+            rows = pl.ds(pl.multiple_of(strip * R, R), R)
+            made.append(wire.copy(stage.at[rows, :], landing.at[here.low], device))
+        return made
+
+    def feed_rows(t):
+        rows = slice(t * MB, (t + 1) * MB)
         branch = dot_nn(att[rows, :], outw[...]) + r.out_bias[...].astype(f32)
         middle = r.tokens_v[rows, :].astype(f32) + mod(2) * branch
         n, inverse = norm_rows(middle)
         modulated = (n * (1.0 + mod(4)) + mod(3)).astype(bf16)
         r.modulated_m[rows, :] = modulated
-
-        def up_chunk(ck, inner):
-            cols = pl.ds(pl.multiple_of(ck * D, D), D)
+        yield
+        for ck in range(chunks):
+            cols = slice(ck * D, (ck + 1) * D)
             u = dot_nn(modulated, upw[:, cols]) + r.up_bias[:, cols].astype(f32)
             phi = 0.5 * (1.0 + lax.erf(u * ROOT_HALF))
             r.activated[rows, cols] = (u * phi).astype(bf16)
-            r.slope[:, cols] = phi + u * (INV_ROOT_2PI * jnp.exp(-0.5 * u * u))
-            return inner
-
-        lax.fori_loop(0, chunks, up_chunk, 0)
+            r.slope[rows, cols] = phi + u * (INV_ROOT_2PI * jnp.exp(-0.5 * u * u))
+            yield
         feed = dot_nn(r.activated[rows, :], downw[...]) + r.down_bias[...].astype(f32)
         r.out_stage[rows, :] = ((middle + mod(5) * feed) * live).astype(bf16)
+        yield
         grad = r.cotangent_v[rows, :].astype(f32) * live
         grad_feed = (grad * mod(5)).astype(bf16)
         r.grad_feed[rows, :] = grad_feed
         acc[5:6, :] += col_sum(grad * feed)
         acc[8:9, :] += col_sum(grad_feed.astype(f32))
-
-        def down_chunk(ck, inner):
-            cols = pl.ds(pl.multiple_of(ck * D, D), D)
-            grad_up = (dot_nt(grad_feed, downw[cols, :]) * r.slope[:, cols]).astype(bf16)
+        yield
+        for ck in range(chunks):
+            cols = slice(ck * D, (ck + 1) * D)
+            grad_up = (dot_nt(grad_feed, downw[cols, :]) * r.slope[rows, cols]).astype(bf16)
             r.grad_up[rows, cols] = grad_up
-            acc[pl.ds(9 + ck, 1), :] += col_sum(grad_up.astype(f32))
-            return inner
-
-        lax.fori_loop(0, chunks, down_chunk, 0)
+            acc[9 + ck : 10 + ck, :] += col_sum(grad_up.astype(f32))
+            yield
         back = dot_nt(r.grad_up[rows, :], upw[...])
         acc[3:4, :] += col_sum(back)
         acc[4:5, :] += col_sum(back * n)
@@ -288,187 +350,239 @@
         grad_branch = (grad_middle * mod(2)).astype(bf16)
         r.grad_branch[rows, :] = grad_branch
         acc[13:14, :] += col_sum(grad_branch.astype(f32))
+        yield
         r.grad_att[rows, :] = dot_nt(grad_branch, outw[...]).astype(bf16)
-        return carry
-
-    lax.fori_loop(0, 2, feed_block, 0)
-
-    def send_back(stage, landing):
-        made = []
-        for i in range(4):
-            strip, device = here.source(i)
-            rows = pl.ds(pl.multiple_of(strip * R, R), R)
-            made.append(wire.copy(stage.at[rows, :], landing.at[here.low], device))
-        return made
-
+
+    blocks = [feed_rows(0), feed_rows(1)]
+    for _ in range(chunks + 2):
+        for block in blocks:
+            next(block)
     out_copies = send_back(r.out_stage, r.out_o)
-
-    part, total = r.part, r.total
-    piece_rows = 4 * D
-    core_rows, plane_rows, z_rows = piece_rows // 2, piece_rows // 8, piece_rows // 32
-    by_core, by_plane, by_z, by_z_back, by_plane_back, by_core_back = {}, {}, {}, {}, {}, {}
-
-    def piece_core(i):
-        base = i * piece_rows
-        src = part.at[pl.ds(pl.multiple_of(base + core_rows * (1 - here.c), core_rows), core_rows), :]
-        by_core[i] = [wire.copy(src, r.land_core.at[i], here.core())]
-
-    def own_core(i):
-        return pl.multiple_of(i * piece_rows + core_rows * here.c, core_rows)
-
-    def piece_plane(i):
-        for made in by_core[i]:
+    for made in cotangent_in:
+        made.wait_recv()
+    for _ in range(chunks + 3):
+        for block in blocks:
+            next(block, None)
+
+    part, total, arena = r.part, r.total, r.arena
+    used = [0]
+    stored = []
+
+    def room(rows):
+        start = used[0]
+        used[0] += rows
+        return start
+
+    def span(start, index, rows):
+        return pl.ds(pl.multiple_of(start + index * rows, 16), rows)
+
+    def wide(ref, rows):
+        return ref[rows, :].astype(f32)
+
+    def receive(flight):
+        for made in flight:
             made.wait_recv()
 
+    def reduce_unit(base, rows, z_first):
+        half = rows // 2
+        land = room(half)
+        block = room(half)
+        flight = [
+            wire.copy(
+                part.at[span(base, 1 - here.c, half), :], arena.at[pl.ds(land, half), :], here.core()
+            )
+        ]
+        yield
+        receive(flight)
+        count = half // 8
+
         def add(q, carry):
-            rows = pl.ds(pl.multiple_of(q * plane_rows, plane_rows), plane_rows)
-            mine = pl.ds(pl.multiple_of(own_core(i) + q * plane_rows, plane_rows), plane_rows)
-            r.sum_core[i, rows, :] = (
-                part[mine, :].astype(f32) + r.land_core[i, rows, :].astype(f32)
+            arena[span(block, q, count), :] = (
+                wide(part, span(base + half * here.c, q, count)) + wide(arena, span(land, q, count))
             ).astype(bf16)
             return carry
 
-        lax.fori_loop(0, 4, add, 0)
-        by_plane[i] = []
-        for k in (3, 1, 2):
-            q, device = here.in_plane(k)
-            rows = pl.ds(pl.multiple_of(q * plane_rows, plane_rows), plane_rows)
-            by_plane[i].append(
-                wire.copy(r.sum_core.at[i, rows, :], r.land_plane.at[i, k - 1], device)
+        lax.fori_loop(0, 8, add, 0)
+        mine = base + half * here.c
+        count = half
+        axes = (here.along_z, here.in_plane) if z_first else (here.in_plane, here.along_z)
+        for axis in axes:
+            count = count // 4
+            land = room(3 * count)
+            flight = []
+            for k in (3, 2, 1):
+                q, device = axis(k)
+                flight.append(
+                    wire.copy(
+                        arena.at[span(block, q, count), :],
+                        arena.at[pl.ds(land + (k - 1) * count, count), :],
+                        device,
+                    )
+                )
+            yield
+            receive(flight)
+            me = axis(0)[0]
+            summed = wide(arena, span(block, me, count)) + wide(arena, pl.ds(land, count))
+            summed = summed + (
+                wide(arena, pl.ds(land + count, count)) + wide(arena, pl.ds(land + 2 * count, count))
             )
-
-    def piece_z(i):
-        for made in by_plane[i]:
-            made.wait_recv()
-        rows = pl.ds(pl.multiple_of(here.plane * plane_rows, plane_rows), plane_rows)
-        summed = r.sum_core[i, rows, :].astype(f32)
-        for k in range(3):
-            summed = summed + r.land_plane[i, k].astype(f32)
-        r.sum_plane[i] = summed.astype(bf16)
-        by_z[i] = []
-        for k in (3, 2, 1):
-            z, device = here.along_z(k)
-            rows = pl.ds(pl.multiple_of(z * z_rows, z_rows), z_rows)
-            by_z[i].append(
-                wire.copy(r.sum_plane.at[i, rows, :], r.land_z.at[i, k - 1], device)
-            )
-
-    def own_plane(i):
-        return pl.multiple_of(own_core(i) + here.plane * plane_rows, plane_rows)
-
-    def piece_z_back(i):
-        for made in by_z[i]:
-            made.wait_recv()
-        rows = pl.ds(pl.multiple_of(here.z * z_rows, z_rows), z_rows)
-        summed = r.sum_plane[i, rows, :].astype(f32)
-        for k in range(3):
-            summed = summed + r.land_z[i, k].astype(f32)
-        mine = pl.ds(pl.multiple_of(own_plane(i) + here.z * z_rows, z_rows), z_rows)
-        total[mine, :] = summed.astype(bf16)
-        by_z_back[i] = [
-            wire.copy(total.at[mine, :], total.at[mine, :], here.along_z(k)[1]) for k in (3, 2, 1)
-        ]
-
-    def piece_plane_back(i):
-        for made in by_z_back[i]:
-            made.wait_recv()
-        mine = pl.ds(own_plane(i), plane_rows)
-        by_plane_back[i] = [
-            wire.copy(total.at[mine, :], total.at[mine, :], here.in_plane(k)[1]) for k in (3, 1, 2)
-        ]
-
-    def piece_core_back(i):
-        for made in by_plane_back[i]:
-            made.wait_recv()
-        mine = pl.ds(own_core(i), core_rows)
-        by_core_back[i] = [wire.copy(total.at[mine, :], total.at[mine, :], here.core())]
-
-    stored = []
-
-    def piece_store(i):
-        for made in by_core_back[i]:
-            made.wait_recv()
-        rows = pl.ds(i * piece_rows, piece_rows)
-        stored.append(local(total.at[rows, :], r.grads_o.at[rows, :]))
-
-    def down_grad(ck, carry):
-        cols = pl.ds(pl.multiple_of(ck * D, D), D)
-        part[cols, :] = dot_tn(r.activated[:, cols], r.grad_feed[...]).astype(bf16)
-        return carry
-
-    lax.fori_loop(0, chunks, down_grad, 0)
-    piece_core(0)
-
-    def up_grad(ck, carry):
-        cols = pl.ds(pl.multiple_of(ck * D, D), D)
-        rows = pl.ds(pl.multiple_of(FF + ck * D, D), D)
-        part[rows, :] = dot_tn(r.modulated_m[...], r.grad_up[:, cols]).astype(bf16)
-        return carry
-
-    lax.fori_loop(0, chunks, up_grad, 0)
-    piece_core(1)
-    piece_plane(0)
+            mine = mine + count * me
+            if axis is axes[0]:
+                block = room(count)
+                arena[pl.ds(block, count), :] = summed.astype(bf16)
+            else:
+                total[span(mine, 0, count), :] = summed.astype(bf16)
+        for axis in axes[::-1]:
+            keep = span(mine, 0, count)
+            flight = [
+                wire.copy(total.at[keep, :], total.at[keep, :], axis(k)[1]) for k in (3, 2, 1)
+            ]
+            yield
+            receive(flight)
+            mine = mine - count * axis(0)[0]
+            count = 4 * count
+        keep = span(mine, 0, half)
+        flight = [wire.copy(total.at[keep, :], total.at[keep, :], here.core())]
+        yield
+        receive(flight)
+        keep = pl.ds(base, rows)
+        stored.append(local(total.at[keep, :], r.grads_o.at[keep, :]))
+        yield
+
+    def reduce_small():
+        small, small_a, small_b, land, small_sum = (
+            r.small,
+            r.small_a,
+            r.small_b,
+            r.land_small,
+            r.small_sum,
+        )
+        here_rows = span(0, here.c, 16)
+        flight = [wire.copy(small.at[span(0, 1 - here.c, 16), :], land.at[0], here.core())]
+        yield
+        receive(flight)
+        small_a[...] = small[here_rows, :] + land[0]
+        flight = [wire.copy(small_a, land.at[k], here.in_plane(k)[1]) for k in (3, 2, 1)]
+        yield
+        receive(flight)
+        small_b[...] = (small_a[...] + land[1]) + (land[2] + land[3])
+        flight = [wire.copy(small_b, land.at[3 + k], here.along_z(k)[1]) for k in (3, 2, 1)]
+        yield
+        receive(flight)
+        small_sum[here_rows, :] = (small_b[...] + land[4]) + (land[5] + land[6])
+        flight = [wire.copy(small_sum.at[here_rows, :], small_sum.at[here_rows, :], here.core())]
+        yield
+        receive(flight)
+        stored.append(local(small_sum, r.small_o))
+        yield
+
+    third = 4 * D // 3
+    early = 2 * FF // EARLY
+    units = [reduce_unit(early * i, early, FORMS[i]) for i in range(EARLY)]
+    units += [reduce_unit(2 * FF + third * i, third, FORMS[EARLY + i]) for i in range(3)]
+    units.append(reduce_small())
+    plan = iter(PLAN)
+
+    def advance():
+        for unit in next(plan):
+            next(units[unit])
+
+    started = 0
+    for ck in range(2 * chunks):
+        rows = slice(ck * D, (ck + 1) * D)
+        cols = slice(ck % chunks * D, (ck % chunks + 1) * D)
+        if ck < chunks:
+            found = dot_tn(r.activated[:, cols], r.grad_feed[...])
+        else:
+            found = dot_tn(r.modulated_m[...], r.grad_up[:, cols])
+        part[rows, :] = found.astype(bf16)
+        while started < EARLY and (started + 1) * early <= (ck + 1) * D:
+            next(units[started])
+            started += 1
+        advance()
     part[2 * FF : 2 * FF + D, :] = dot_tn(att[...], r.grad_branch[...]).astype(bf16)
 
     gat, qgt = r.gat, r.qgt
     for p in range(pairs):
         gat[p * 128 : (p + 1) * 128, :] = r.grad_att[:, p * 128 : (p + 1) * 128].T.astype(f32)
     zero_half = jnp.zeros((HEAD_DIM, QB), bf16)
-    gst, gstt, deltas, dss = r.gst, r.gstt, r.deltas, r.dss
-    dkv = r.dkv
-    dkv_copies = []
-    other = pl.multiple_of((1 - here.rows_half) * M, M)
+    gst, gstt, deltas, dkv = r.gst, r.gstt, r.deltas, r.dkv
+    dss = (r.dss_a, r.dss_b)
     for p in range(pairs):
         for qb in range(4):
             half = qb // 2
-            head = p * 128 + half * HEAD_DIM
-            queries = slice((qb % 2) * QB, (qb % 2) * QB + QB)
-            inv = r.inv_sum[4 * p + qb]
-            scaled = gat[head : head + HEAD_DIM, queries] * inv
-            deltas[qb] = col_sum(scaled * ots[head : head + HEAD_DIM, queries])
+            head = slice(p * 128 + half * HEAD_DIM, p * 128 + (half + 1) * HEAD_DIM)
+            queries = slice(qb % 2 * QB, (qb % 2 + 1) * QB)
+            scaled = gat[head, queries] * r.inv_sum[4 * p + qb]
+            deltas[4 * p + qb] = col_sum(scaled * ots[head, queries])
             scaled = scaled.astype(bf16)
             filled = [scaled, zero_half] if half == 0 else [zero_half, scaled]
-            gstt[:, qb * QB : (qb + 1) * QB] = jnp.concatenate(filled, axis=0)
-        gst[...] = gstt[...].T
-
-        def backward_block(qb, carry, p=p):
-            queries = pl.ds(pl.multiple_of(qb * QB, QB), QB)
-            slope = dot_nn(kv[:, D + p * 128 : D + (p + 1) * 128], gstt[:, queries])
-            grad_scores = (es[p, :, queries].astype(f32) * (slope - deltas[qb])).astype(bf16)
-            dss[:, queries] = grad_scores
-            head = pl.multiple_of(p * 128 + (qb // 2) * HEAD_DIM, HEAD_DIM)
-            grad_q = dot_nn(kvt[pl.ds(head, HEAD_DIM), :], grad_scores) * HEAD_DIM ** (-0.5)
-            qgt[pl.ds(head, HEAD_DIM), pl.ds(pl.multiple_of((qb % 2) * QB, QB), QB)] = grad_q
-            return carry
-
-        lax.fori_loop(0, 4, backward_block, 0)
-        dkv[p, :, 0:128] = dot_nn(dss[...], qst[p]).astype(bf16)
-        dkv[p, :, 128:256] = dot_nn(es[p], gst[...]).astype(bf16)
-        dkv_copies.append(wire.copy(dkv.at[p, pl.ds(other, M), :], r.land_dkv.at[p], here.core()))
-        if p == 0:
-            piece_plane(1)
-            piece_z(0)
-        if p == 1:
-            piece_z(1)
-            piece_z_back(0)
+            gstt[p, :, qb * QB : (qb + 1) * QB] = jnp.concatenate(filled, axis=0)
+        gst[p] = gstt[p].T
+    other = pl.multiple_of((1 - here.rows_half) * M, M)
+    dkv_copies = []
     gp = r.grad_projected
+
+    def finish_pair(p):
+        gp[p, :, 0:128] = qgt[p * 128 : (p + 1) * 128, :].T.astype(bf16)
+        dkv_copies[p].wait_recv()
+        gp[p, :, 128:384] = (
+            dkv[p, pl.ds(own, M), :].astype(f32) + r.land_dkv[p].astype(f32)
+        ).astype(bf16)
+        rows = slice(2 * FF + (p + 1) * D, 2 * FF + (p + 2) * D)
+        part[rows, :] = dot_tn(r.modulated[...], gp[p]).astype(bf16)
+        next(units[EARLY + p])
+        advance()
+
+    def grad_values(p, c):
+        keys = slice(c * CB, (c + 1) * CB)
+        dkv[p, keys, 128:256] = dot_nn(es[p, keys, :], gst[p]).astype(bf16)
+
+    def grad_keys(p, c):
+        keys = slice(c * CB, (c + 1) * CB)
+        dkv[p, keys, 0:128] = dot_nn(dss[p % 2][keys, :], qst[p]).astype(bf16)
+        if c == 3:
+            dkv_copies.append(
+                wire.copy(dkv.at[p, pl.ds(other, M), :], r.land_dkv.at[p], here.core())
+            )
+
+    def grad_queries(p, qb):
+        half = qb // 2 * HEAD_DIM
+        head = slice(p * 128 + half, p * 128 + half + HEAD_DIM)
+        found = dot_nn(kvt[p, half : half + HEAD_DIM, :], dss[p % 2][:, qb * QB : (qb + 1) * QB])
+        qgt[head, qb % 2 * QB : (qb % 2 + 1) * QB] = found * HEAD_DIM ** (-0.5)
+
+    later = []
+    advance()
     for p in range(pairs):
-        cols = slice(p * 128, (p + 1) * 128)
-        gp[:, cols] = qgt[cols, :].T.astype(bf16)
-        dkv_copies[p].wait_recv()
-        summed = dkv[p, pl.ds(own, M), :].astype(f32) + r.land_dkv[p].astype(f32)
-        gp[:, D + p * 128 : D + (p + 1) * 128] = summed[:, :128].astype(bf16)
-        gp[:, 2 * D + p * 128 : 2 * D + (p + 1) * 128] = summed[:, 128:].astype(bf16)
-
-    for b in range(3):
-        cols = slice(b * D, (b + 1) * D)
-        rows = slice(2 * FF + (b + 1) * D, 2 * FF + (b + 2) * D)
-        part[rows, :] = dot_tn(r.modulated[...], gp[:, cols]).astype(bf16)
-    piece_core(2)
-
-    def token_block(t, carry):
-        rows = pl.ds(pl.multiple_of(t * MB, MB), MB)
-        back = dot_nt(gp[rows, :], r.qkv_weight_v[...])
+        for qb in range(4):
+            queries = slice(qb * QB, (qb + 1) * QB)
+            for c in range(4):
+                keys = slice(c * CB, (c + 1) * CB)
+                slope = dot_nn(kv[p, keys, 128:], gstt[p, :, queries])
+                dss[p % 2][keys, queries] = (
+                    es[p, keys, queries].astype(f32) * (slope - deltas[4 * p + qb])
+                ).astype(bf16)
+                if later:
+                    later.pop(0)()
+            later.append(functools.partial(grad_queries, p, qb))
+            if qb == 0:
+                later += [functools.partial(grad_values, p, k) for k in range(4)]
+            if qb == 3:
+                later += [functools.partial(grad_keys, p, k) for k in range(4)]
+            advance()
+            if p > 0 and qb == 3:
+                finish_pair(p - 1)
+    for made in later:
+        made()
+    advance()
+    finish_pair(pairs - 1)
+
+    for t in range(2):
+        rows = slice(t * MB, (t + 1) * MB)
+        back = dot_nt(gp[0, rows, :], r.qkv_weight_v[0])
+        for p in range(1, pairs):
+            back = back + dot_nt(gp[p, rows, :], r.qkv_weight_v[p])
         n = r.normed[rows, :]
         acc[0:1, :] += col_sum(back)
         acc[1:2, :] += col_sum(back * n)
@@ -476,53 +590,16 @@
             back * (1.0 + mod(1)), n, r.inverse[rows, :]
         )
         r.gtok_stage[rows, :] = grad.astype(bf16)
-        return carry
-
-    lax.fori_loop(0, 2, token_block, 0)
-    piece_plane(2)
+        if t == 0:
+            advance()
     gtok_copies = send_back(r.gtok_stage, r.gtok_o)
 
     small = r.small
     for k in range(6):
         small[4 * k : 4 * k + 4, :] = onehot * acc[k : k + 1, :]
     small[24:32, :] = acc[8:16, :]
-    rows_here = pl.ds(pl.multiple_of(16 * here.c, 16), 16)
-    rows_there = pl.ds(pl.multiple_of(16 * (1 - here.c), 16), 16)
-    flight = wire.copy(small.at[rows_there, :], r.land_small.at[0], here.core())
-    flight.wait_recv()
-    r.small_a[...] = small[rows_here, :] + r.land_small[0]
-    flight = [
-        wire.copy(r.small_a, r.land_small.at[k], here.in_plane(k)[1]) for k in (3, 1, 2)
-    ]
-    piece_z_back(1)
-    for made in flight:
-        made.wait_recv()
-    r.small_b[...] = (
-        r.small_a[...] + r.land_small[1] + r.land_small[2] + r.land_small[3]
-    )
-    flight = [
-        wire.copy(r.small_b, r.land_small.at[3 + k], here.along_z(k)[1]) for k in (3, 2, 1)
-    ]
-    piece_plane_back(0)
-    piece_z(2)
-    piece_plane_back(1)
-    for made in flight:
-        made.wait_recv()
-    small_sum = r.small_sum
-    small_sum[rows_here, :] = (
-        r.small_b[...] + r.land_small[4] + r.land_small[5] + r.land_small[6]
-    )
-    flight = wire.copy(small_sum.at[rows_here, :], small_sum.at[rows_here, :], here.core())
-    piece_core_back(0)
-    piece_z_back(2)
-    piece_core_back(1)
-    flight.wait_recv()
-    stored.append(local(small_sum, r.small_o))
-    piece_store(0)
-    piece_plane_back(2)
-    piece_store(1)
-    piece_core_back(2)
-    piece_store(2)
+    next(units[EARLY + 3])
+    advance()
     for made in out_copies + gtok_copies:
         made.wait_recv()
     wire.finish()
@@ -602,9 +679,11 @@
     grads_in[2].wait()
     r.gout_v[...] = grads[2 * FF : 2 * FF + D, :].astype(f32)
     outs.append(local(r.gout_v, r.gout.at[0]))
-    for k in range(3):
-        rows = slice(2 * FF + (k + 1) * D, 2 * FF + (k + 2) * D)
-        r.gqkv_v[:, k * D : (k + 1) * D] = grads[rows, :].astype(f32)
+    for p in range(D // 128):
+        for k in range(3):
+            rows = slice(2 * FF + (p + 1) * D, 2 * FF + (p + 2) * D)
+            cols = slice(k * D + p * 128, k * D + (p + 1) * 128)
+            r.gqkv_v[:, cols] = grads[rows, k * 128 : (k + 1) * 128].astype(f32)
     outs.append(local(r.gqkv_v, r.gqkv.at[0]))
     for made in outs:
         made.wait()
@@ -636,10 +715,9 @@
         lead_class=smem,
         group_count=smem,
     )
-    piece = 4 * D
     scratch = dict(
         ada_weight_v=pltpu.VMEM((D, 6 * D), bf16),
-        qkv_weight_v=pltpu.VMEM((D, 3 * D), bf16),
+        qkv_weight_v=pltpu.VMEM((pairs, D, 384), bf16),
         out_weight_v=pltpu.VMEM((D, D), bf16),
         up_weight_v=pltpu.VMEM((D, FF), bf16),
         down_weight_v=pltpu.VMEM((FF, D), bf16),
@@ -650,8 +728,8 @@
         normed=pltpu.VMEM((M, D), f32),
         inverse=pltpu.VMEM((M, 1), f32),
         modulated=pltpu.VMEM((M, D), bf16),
-        kv=pltpu.VMEM((N, 2 * D), bf16),
-        kvt=pltpu.VMEM((2 * D, N), bf16),
+        kv=pltpu.VMEM((pairs, N, 256), bf16),
+        kvt=pltpu.VMEM((pairs, 256, N), bf16),
         qst=pltpu.VMEM((pairs, 2 * M, 128), bf16),
         es=pltpu.VMEM((pairs, N, 2 * M), bf16),
         inv_sum=pltpu.VMEM((4 * pairs, 1, M // 2), f32),
@@ -659,7 +737,7 @@
         att=pltpu.VMEM((M, D), bf16),
         modulated_m=pltpu.VMEM((M, D), bf16),
         activated=pltpu.VMEM((M, FF), bf16),
-        slope=pltpu.VMEM((M // 2, FF), f32),
+        slope=pltpu.VMEM((M, FF), f32),
         out_stage=pltpu.VMEM((M, D), bf16),
         grad_feed=pltpu.VMEM((M, D), bf16),
         grad_up=pltpu.VMEM((M, FF), bf16),
@@ -668,29 +746,28 @@
         grad_att=pltpu.VMEM((M, D), bf16),
         gat=pltpu.VMEM((D, M), f32),
         qgt=pltpu.VMEM((D, M), f32),
-        gst=pltpu.VMEM((2 * M, 128), bf16),
-        gstt=pltpu.VMEM((128, 2 * M), bf16),
-        deltas=pltpu.VMEM((4, 1, M // 2), f32),
-        dss=pltpu.VMEM((N, 2 * M), bf16),
+        gst=pltpu.VMEM((pairs, 2 * M, 128), bf16),
+        gstt=pltpu.VMEM((pairs, 128, 2 * M), bf16),
+        deltas=pltpu.VMEM((4 * pairs, 1, M // 2), f32),
+        dss_a=pltpu.VMEM((N, 2 * M), bf16),
+        dss_b=pltpu.VMEM((N, 2 * M), bf16),
+        scores_a=pltpu.VMEM((N, M // 2), f32),
+        scores_b=pltpu.VMEM((N, M // 2), f32),
         dkv=pltpu.VMEM((pairs, N, 256), bf16),
         land_dkv=pltpu.VMEM((pairs, M, 256), bf16),
-        grad_projected=pltpu.VMEM((M, 3 * D), bf16),
+        grad_projected=pltpu.VMEM((pairs, M, 384), bf16),
         gtok_stage=pltpu.VMEM((M, D), bf16),
         part=pltpu.VMEM((total_rows, D), bf16),
         total=pltpu.VMEM((total_rows, D), bf16),
-        land_core=pltpu.VMEM((3, piece // 2, D), bf16),
-        sum_core=pltpu.VMEM((3, piece // 2, D), bf16),
-        land_plane=pltpu.VMEM((3, 3, piece // 8, D), bf16),
-        sum_plane=pltpu.VMEM((3, piece // 8, D), bf16),
-        land_z=pltpu.VMEM((3, 3, piece // 32, D), bf16),
+        arena=pltpu.VMEM((2 * total_rows, D), bf16),
         small=pltpu.VMEM((32, D), f32),
         small_a=pltpu.VMEM((16, D), f32),
         small_b=pltpu.VMEM((16, D), f32),
         small_sum=pltpu.VMEM((32, D), f32),
         land_small=pltpu.VMEM((7, 16, D), f32),
-        send_sems=pltpu.SemaphoreType.DMA((80,)),
-        recv_sems=pltpu.SemaphoreType.DMA((80,)),
-        local_sems=pltpu.SemaphoreType.DMA((12,)),
+        send_sems=pltpu.SemaphoreType.DMA((176,)),
+        recv_sems=pltpu.SemaphoreType.DMA((176,)),
+        local_sems=pltpu.SemaphoreType.DMA((24,)),
     )
     mids = dict(
         out_o=jax.ShapeDtypeStruct((4, R, D), bf16),

time: 118 us -> 96.4 us (0.82)
  Pallas kernels: 117 us -> 95.3 us
    pallas_call x1, Pallas kernels: 108 us -> 87 us  [fast_body(): pl.pallas_call(functools.partial(main_kernel, (R, D, FF), names), out_sha...]
where the time goes in v2:
time: 96.4 us; the launch traced here: 96.2 us
  Pallas kernels  95.3 us (99%)
    pallas_call x1, Pallas kernels, fast_body(): pl.pallas_call(functools.partial(main_kernel, (R, D, FF), names), out_sha...  87 us
    pallas_call x1, Pallas kernels, fast_body(): pl.pallas_call(functools.partial(last_kernel, (D, FF), names), out_shape=...  8.34 us

profile of v2, /device:TPU:9, one launch (start us, length us, event | category | flops | bytes accessed | tf_op | source)
XLA Modules:
  0.0 96.2 jit_solution(4709464038632817127)
XLA Ops:
  0.6 87.0 %block_forward_backward.1 = (bf16[4,128,384]{2,1,0:T(8,128)(2,1)}, bf16[4,128,384]{2,1,0:T(8,128)(2,1)}, bf16[4608,384]{1,0:T(8,128)(2,1)}, f32[32,384]{1,0:T(8,128)}) custom-call(bf16[1,4,128,384]{3,2,1,0:T(8,128)(2,1)} %refs_0_.1, bf16[1,4,128,384]{3,2,1,0:T(8,128)(2,1)} %refs_1_.1, bf16[4,384]{1,0:T(4,128)(2,1)} %refs_4_.3, ...), custom_call_target="tpu_custom_call" | custom-call | tf_op jit(solution)/shard_map/block_forward_backward/pallas_call | solution.py:779
  87.7 8.3 %widen_and_embed.1 = (f32[1,4,128,384]{3,2,1,0:T(8,128)}, f32[1,4,128,384]{3,2,1,0:T(8,128)}, f32[4,384]{1,0:T(4,128)}, f32[1,384,2304]{2,1,0:T(8,128)}, f32[1,2...) custom-call(bf16[4,128,384]{2,1,0:T(8,128)(2,1)} %get-tuple-element., ...), custom_call_target="tpu_custom_call" | custom-call | tf_op jit(solution)/shard_map/widen_and_embed/pallas_call | solution.py:828

commit v3 on v2

--- a/solution.py
+++ b/solution.py
@@ -14,36 +14,38 @@
 ROOT_HALF = 0.7071067811865476
 INV_ROOT_2PI = 0.3989422804014327
 HEAD_DIM = 64
+EARLY_COTANGENT = 0
 EARLY = 6
 FORMS = (False, False, False, False, False, False, False, False, False)
 PLAN = (
-    (),
-    (),
-    (),
-    (),
-    (),
-    (0, 1),
-    (2, 3),
-    (),
-    (4,),
-    (5,),
+    (12, 13, 10, 11),
+    (),
+    (),
+    (),
+    (),
+    (),
+    (),
     (),
     (0,),
-    (),
+    (1, 2),
+    (3, 4, 5),
+    (),
+    (),
+    (),
+    (),
+    (),
+    (),
+    (0,),
     (),
     (1,),
     (),
     (),
-    (2, 0),
-    (),
-    (3, 6, 1),
-    (),
-    (4,),
-    (),
-    (2, 5),
-    (0, 7, 3, 6, 1, 4, 8),
+    (6, 2),
+    (),
+    (0, 3),
+    (7, 4, 1),
     (2,),
-    (5, 9, 3, 0, 6, 0, 4, 7, 1, 1, 8, 2, 2, 5, 6, 7, 9, 8, 3, 3, 4, 7, 4, 5, 9, 5, 8, 9, 6, 6, 7, 7, 8, 8),
+    (5, 15, 8, 0, 6, 9, 3, 4, 7, 1, 2, 5, 8, 6, 0, 3, 9, 0, 4, 7, 1, 5, 1, 8, 2, 14, 16, 6, 2, 3, 9, 3, 7, 9, 4, 8, 4, 17, 5, 5, 6, 6, 7, 7, 8, 8),
 )
 
 
@@ -121,31 +123,29 @@
 class Wire:
     def __init__(self, send_sems, recv_sems):
         self.send_sems, self.recv_sems = send_sems, recv_sems
-        self.count = 0
-        self.sent = []
-
-    def copy(self, src, dst, device):
-        index = self.count
-        self.count += 1
-        made = pltpu.make_async_remote_copy(
+        self.outs, self.ins = 0, 0
+
+    def sender(self):
+        self.outs += 1
+        return self.send_sems.at[self.outs - 1]
+
+    def receiver(self):
+        self.ins += 1
+        return self.recv_sems.at[self.ins - 1]
+
+    def copy(self, src, dst, device, sender, receiver):
+        pltpu.make_async_remote_copy(
             src_ref=src,
             dst_ref=dst,
-            send_sem=self.send_sems.at[index],
-            recv_sem=self.recv_sems.at[index],
+            send_sem=sender,
+            recv_sem=receiver,
             device_id=device,
             device_id_type=MESH,
-        )
-        made.start()
-        self.sent.append(made)
-        return made
-
-    def sent_out(self, made):
-        made.wait_send()
-        self.sent.remove(made)
-
-    def finish(self):
-        for made in self.sent:
-            made.wait_send()
+        ).start()
+
+
+def take(semaphore, like):
+    pltpu.make_async_copy(like, like, semaphore).wait()
 
 
 def main_kernel(sizes, names, *refs):
@@ -165,15 +165,23 @@
         made.start()
         return made
 
+    small_loads = [
+        local(r.emb_table, r.emb_table_v),
+        local(r.ada_bias, r.ada_bias_v),
+        local(r.out_bias, r.out_bias_v),
+        local(r.up_bias, r.up_bias_v),
+        local(r.down_bias, r.down_bias_v),
+    ]
     load_ada = local(r.ada_weight.at[0], r.ada_weight_v)
-    load_qkv = [
-        local(
-            r.qkv_weight.at[0, :, pl.ds(b * D + p * 128, 128)],
-            r.qkv_weight_v.at[p, :, pl.ds(b * 128, 128)],
-        )
-        for p in range(pairs)
-        for b in range(3)
-    ]
+    qkv_sem = local_sems.at[local_count[0]]
+    local_count[0] += 1
+    for p in range(pairs):
+        for b in range(3):
+            pltpu.make_async_copy(
+                r.qkv_weight.at[0, :, pl.ds(b * D + p * 128, 128)],
+                r.qkv_weight_v.at[p, :, pl.ds(b * 128, 128)],
+                qkv_sem,
+            ).start()
     load_rest = [
         local(r.out_weight.at[0], r.out_weight_v),
         local(r.up_weight.at[0], r.up_weight_v),
@@ -188,20 +196,22 @@
         pl.semaphore_signal(barrier, inc=1, device_id=device, device_id_type=MESH)
     pl.semaphore_wait(barrier, len(partners))
 
-    def send_home(whole, landing):
+    def send_home(whole, landing, i, sender, receiver):
         place = pl.ds(pl.multiple_of(here.low * R, R), R)
-        made = []
-        for i in range(4):
-            slot, device = here.home(i)
-            made.append(wire.copy(whole.at[0, slot], landing.at[place, :], device))
-        return made
-
-    tokens_in = send_home(r.tokens, r.tokens_v)
+        slot, device = here.home(i)
+        wire.copy(whole.at[0, slot], landing.at[place, :], device, sender, receiver)
+
+    tokens_out, tokens_in = wire.sender(), [wire.receiver() for _ in range(4)]
+    cotangent_out, cotangent_in = wire.sender(), wire.receiver()
+    for i in range(4):
+        send_home(r.tokens, r.tokens_v, i, tokens_out, tokens_in[i])
 
     group, slot = 2 * here.y + here.half, here.low
     item_class = r.lead_class[group, slot]
     live = (slot < r.group_count[group]).astype(f32)
-    table = r.emb_table[...].astype(f32)
+    for made in small_loads:
+        made.wait()
+    table = r.emb_table_v[...].astype(f32)
     class_col = lax.broadcasted_iota(jnp.int32, (table.shape[0], 1), 0)
     onehot = (class_col == item_class).astype(f32)
     embed = jnp.sum(onehot * table, axis=0, keepdims=True)
@@ -217,7 +227,7 @@
         cols = pl.ds(k * D, D)
         mods[k : k + 1, :] = col_sum(
             dot_nn(parts.astype(bf16), r.ada_weight_v[:, cols])
-        ) + r.ada_bias[:, cols].astype(f32)
+        ) + r.ada_bias_v[:, cols].astype(f32)
 
     def mod(k):
         return mods[k : k + 1, :]
@@ -225,16 +235,15 @@
     acc = r.acc
     acc[...] = jnp.zeros_like(acc)
 
-    for made in load_qkv:
-        made.wait()
+    take(qkv_sem, r.qkv_weight_v)
     lane = lax.broadcasted_iota(jnp.int32, (R, 128), 1)
     left = lane < HEAD_DIM
     kv, qst = r.kv, r.qst
-    kv_copies = []
+    kv_out, kv_in = wire.sender(), wire.receiver()
     own = pl.multiple_of(here.rows_half * M, M)
     for i in range(4):
         strip, _ = here.source(i)
-        tokens_in[i].wait_recv()
+        take(tokens_in[i], r.tokens_v.at[pl.ds(0, R), :])
         at = pl.multiple_of(strip * R, R)
         rows = pl.ds(at, R)
         normed, inverse = norm_rows(r.tokens_v[rows, :].astype(f32))
@@ -250,12 +259,13 @@
             zero = jnp.zeros_like(q)
             qst[p, pl.ds(at, R), :] = jnp.where(left, q, zero)
             qst[p, pl.ds(pl.multiple_of(M + at, R), R), :] = jnp.where(left, zero, q)
-        kv_copies.append(wire.copy(kv.at[:, kv_rows, :], kv.at[:, kv_rows, :], here.core()))
-    for made in tokens_in:
-        wire.sent_out(made)
-    cotangent_in = send_home(r.cotangent, r.cotangent_v)
-    for made in kv_copies:
-        made.wait_recv()
+        wire.copy(kv.at[:, kv_rows, :], kv.at[:, kv_rows, :], here.core(), kv_out, kv_in)
+        if i < EARLY_COTANGENT:
+            send_home(r.cotangent, r.cotangent_v, i, cotangent_out, cotangent_in)
+    take(tokens_out, r.tokens_v)
+    for i in range(EARLY_COTANGENT, 4):
+        send_home(r.cotangent, r.cotangent_v, i, cotangent_out, cotangent_in)
+    take(kv_in, kv.at[:, pl.ds(0, M), :])
 
     kvt, es, ots = r.kvt, r.es, r.ots
     for p in range(pairs):
@@ -298,22 +308,162 @@
     for p in range(pairs):
         att[:, p * 128 : (p + 1) * 128] = ots[p * 128 : (p + 1) * 128, :].T.astype(bf16)
 
+    part, total, arena = r.part, r.total, r.arena
+    used = [0]
+    stored = []
+
+    def room(rows):
+        start = used[0]
+        used[0] += rows
+        return start
+
+    def span(start, index, rows):
+        return pl.ds(pl.multiple_of(start + index * rows, 16), rows)
+
+    def wide(ref, rows):
+        return ref[rows, :].astype(f32)
+
+    units_out = wire.sender()
+    units_rows = [0]
+
+    def reduce_unit(base, rows, z_first):
+        half = rows // 2
+
+        def move(src, dst, device, receiver):
+            units_rows[0] += src.shape[0]
+            wire.copy(src, dst, device, units_out, receiver)
+
+        land = room(half)
+        block = room(half)
+        arrived = wire.receiver()
+        move(
+            part.at[span(base, 1 - here.c, half), :],
+            arena.at[pl.ds(land, half), :],
+            here.core(),
+            arrived,
+        )
+        yield
+        take(arrived, arena.at[pl.ds(land, half), :])
+        arena[pl.ds(block, half), :] = (
+            wide(part, span(base, here.c, half)) + wide(arena, pl.ds(land, half))
+        ).astype(bf16)
+        mine = base + half * here.c
+        count = half
+        axes = (here.along_z, here.in_plane) if z_first else (here.in_plane, here.along_z)
+        for axis in axes:
+            count = count // 4
+            land = room(3 * count)
+            arrived = wire.receiver()
+            for k in (3, 2, 1):
+                q, device = axis(k)
+                move(
+                    arena.at[span(block, q, count), :],
+                    arena.at[pl.ds(land + (k - 1) * count, count), :],
+                    device,
+                    arrived,
+                )
+            yield
+            take(arrived, arena.at[pl.ds(land, 3 * count), :])
+            me = axis(0)[0]
+            summed = wide(arena, span(block, me, count)) + wide(arena, pl.ds(land, count))
+            summed = summed + (
+                wide(arena, pl.ds(land + count, count)) + wide(arena, pl.ds(land + 2 * count, count))
+            )
+            mine = mine + count * me
+            if axis is axes[0]:
+                block = room(count)
+                arena[pl.ds(block, count), :] = summed.astype(bf16)
+            else:
+                total[span(mine, 0, count), :] = summed.astype(bf16)
+        for axis in axes[::-1]:
+            keep = span(mine, 0, count)
+            arrived = wire.receiver()
+            for k in (3, 2, 1):
+                move(total.at[keep, :], total.at[keep, :], axis(k)[1], arrived)
+            yield
+            take(arrived, total.at[pl.ds(0, 3 * count), :])
+            mine = mine - count * axis(0)[0]
+            count = 4 * count
+        keep = span(mine, 0, half)
+        arrived = wire.receiver()
+        move(total.at[keep, :], total.at[keep, :], here.core(), arrived)
+        yield
+        take(arrived, total.at[pl.ds(0, half), :])
+        keep = pl.ds(base, rows)
+        stored.append(local(total.at[keep, :], r.grads_o.at[keep, :]))
+        yield
+
+    small_out = wire.sender()
+
+    def reduce_small():
+        small, small_a, small_b, land, small_sum = (
+            r.small,
+            r.small_a,
+            r.small_b,
+            r.land_small,
+            r.small_sum,
+        )
+        here_rows = span(0, here.c, 16)
+        arrived = wire.receiver()
+        wire.copy(small.at[span(0, 1 - here.c, 16), :], land.at[0], here.core(), small_out, arrived)
+        yield
+        take(arrived, land.at[0])
+        small_a[...] = small[here_rows, :] + land[0]
+        arrived = wire.receiver()
+        for k in (3, 2, 1):
+            wire.copy(small_a, land.at[k], here.in_plane(k)[1], small_out, arrived)
+        yield
+        take(arrived, land.at[pl.ds(1, 3)])
+        small_b[...] = (small_a[...] + land[1]) + (land[2] + land[3])
+        arrived = wire.receiver()
+        for k in (3, 2, 1):
+            wire.copy(small_b, land.at[3 + k], here.along_z(k)[1], small_out, arrived)
+        yield
+        take(arrived, land.at[pl.ds(4, 3)])
+        small_sum[here_rows, :] = (small_b[...] + land[4]) + (land[5] + land[6])
+        arrived = wire.receiver()
+        wire.copy(
+            small_sum.at[here_rows, :], small_sum.at[here_rows, :], here.core(), small_out, arrived
+        )
+        yield
+        take(arrived, small_sum.at[pl.ds(0, 16), :])
+        stored.append(local(small_sum, r.small_o))
+        yield
+
+    def send_back(stage, landing, i, sender, receiver):
+        strip, device = here.source(i)
+        rows = pl.ds(pl.multiple_of(strip * R, R), R)
+        wire.copy(stage.at[rows, :], landing.at[here.low], device, sender, receiver)
+        yield
+
+    out_out, out_in, gtok_out, gtok_in = (
+        wire.sender(),
+        wire.receiver(),
+        wire.sender(),
+        wire.receiver(),
+    )
+
+    third = 4 * D // 3
+    early = 2 * FF // EARLY
+    units = [reduce_unit(early * i, early, FORMS[i]) for i in range(EARLY)]
+    units += [reduce_unit(2 * FF + third * i, third, FORMS[EARLY + i]) for i in range(3)]
+    units.append(reduce_small())
+    units += [send_back(r.out_stage, r.out_o, i, out_out, out_in) for i in range(4)]
+    units += [send_back(r.gtok_stage, r.gtok_o, i, gtok_out, gtok_in) for i in range(4)]
+    plan = iter(PLAN)
+
+    def advance():
+        for unit in next(plan):
+            next(units[unit])
+
     for made in load_rest:
         made.wait()
     outw, upw, downw = r.out_weight_v, r.up_weight_v, r.down_weight_v
     chunks = FF // D
 
-    def send_back(stage, landing):
-        made = []
-        for i in range(4):
-            strip, device = here.source(i)
-            rows = pl.ds(pl.multiple_of(strip * R, R), R)
-            made.append(wire.copy(stage.at[rows, :], landing.at[here.low], device))
-        return made
-
     def feed_rows(t):
         rows = slice(t * MB, (t + 1) * MB)
-        branch = dot_nn(att[rows, :], outw[...]) + r.out_bias[...].astype(f32)
+        branch = dot_nn(att[rows, :], outw[...]) + r.out_bias_v[...].astype(f32)
         middle = r.tokens_v[rows, :].astype(f32) + mod(2) * branch
         n, inverse = norm_rows(middle)
         modulated = (n * (1.0 + mod(4)) + mod(3)).astype(bf16)
@@ -321,12 +471,12 @@
         yield
         for ck in range(chunks):
             cols = slice(ck * D, (ck + 1) * D)
-            u = dot_nn(modulated, upw[:, cols]) + r.up_bias[:, cols].astype(f32)
+            u = dot_nn(modulated, upw[:, cols]) + r.up_bias_v[:, cols].astype(f32)
             phi = 0.5 * (1.0 + lax.erf(u * ROOT_HALF))
             r.activated[rows, cols] = (u * phi).astype(bf16)
             r.slope[rows, cols] = phi + u * (INV_ROOT_2PI * jnp.exp(-0.5 * u * u))
             yield
-        feed = dot_nn(r.activated[rows, :], downw[...]) + r.down_bias[...].astype(f32)
+        feed = dot_nn(r.activated[rows, :], downw[...]) + r.down_bias_v[...].astype(f32)
         r.out_stage[rows, :] = ((middle + mod(5) * feed) * live).astype(bf16)
         yield
         grad = r.cotangent_v[rows, :].astype(f32) * live
@@ -357,135 +507,11 @@
     for _ in range(chunks + 2):
         for block in blocks:
             next(block)
-    out_copies = send_back(r.out_stage, r.out_o)
-    for made in cotangent_in:
-        made.wait_recv()
+    advance()
+    take(cotangent_in, r.cotangent_v)
     for _ in range(chunks + 3):
         for block in blocks:
             next(block, None)
-
-    part, total, arena = r.part, r.total, r.arena
-    used = [0]
-    stored = []
-
-    def room(rows):
-        start = used[0]
-        used[0] += rows
-        return start
-
-    def span(start, index, rows):
-        return pl.ds(pl.multiple_of(start + index * rows, 16), rows)
-
-    def wide(ref, rows):
-        return ref[rows, :].astype(f32)
-
-    def receive(flight):
-        for made in flight:
-            made.wait_recv()
-
-    def reduce_unit(base, rows, z_first):
-        half = rows // 2
-        land = room(half)
-        block = room(half)
-        flight = [
-            wire.copy(
-                part.at[span(base, 1 - here.c, half), :], arena.at[pl.ds(land, half), :], here.core()
-            )
-        ]
-        yield
-        receive(flight)
-        count = half // 8
-
-        def add(q, carry):
-            arena[span(block, q, count), :] = (
-                wide(part, span(base + half * here.c, q, count)) + wide(arena, span(land, q, count))
-            ).astype(bf16)
-            return carry
-
-        lax.fori_loop(0, 8, add, 0)
-        mine = base + half * here.c
-        count = half
-        axes = (here.along_z, here.in_plane) if z_first else (here.in_plane, here.along_z)
-        for axis in axes:
-            count = count // 4
-            land = room(3 * count)
-            flight = []
-            for k in (3, 2, 1):
-                q, device = axis(k)
-                flight.append(
-                    wire.copy(
-                        arena.at[span(block, q, count), :],
-                        arena.at[pl.ds(land + (k - 1) * count, count), :],
-                        device,
-                    )
-                )
-            yield
-            receive(flight)
-            me = axis(0)[0]
-            summed = wide(arena, span(block, me, count)) + wide(arena, pl.ds(land, count))
-            summed = summed + (
-                wide(arena, pl.ds(land + count, count)) + wide(arena, pl.ds(land + 2 * count, count))
-            )
-            mine = mine + count * me
-            if axis is axes[0]:
-                block = room(count)
-                arena[pl.ds(block, count), :] = summed.astype(bf16)
-            else:
-                total[span(mine, 0, count), :] = summed.astype(bf16)
-        for axis in axes[::-1]:
-            keep = span(mine, 0, count)
-            flight = [
-                wire.copy(total.at[keep, :], total.at[keep, :], axis(k)[1]) for k in (3, 2, 1)
-            ]
-            yield
-            receive(flight)
-            mine = mine - count * axis(0)[0]
-            count = 4 * count
-        keep = span(mine, 0, half)
-        flight = [wire.copy(total.at[keep, :], total.at[keep, :], here.core())]
-        yield
-        receive(flight)
-        keep = pl.ds(base, rows)
-        stored.append(local(total.at[keep, :], r.grads_o.at[keep, :]))
-        yield
-
-    def reduce_small():
-        small, small_a, small_b, land, small_sum = (
-            r.small,
-            r.small_a,
-            r.small_b,
-            r.land_small,
-            r.small_sum,
-        )
-        here_rows = span(0, here.c, 16)
-        flight = [wire.copy(small.at[span(0, 1 - here.c, 16), :], land.at[0], here.core())]
-        yield
-        receive(flight)
-        small_a[...] = small[here_rows, :] + land[0]
-        flight = [wire.copy(small_a, land.at[k], here.in_plane(k)[1]) for k in (3, 2, 1)]
-        yield
-        receive(flight)
-        small_b[...] = (small_a[...] + land[1]) + (land[2] + land[3])
-        flight = [wire.copy(small_b, land.at[3 + k], here.along_z(k)[1]) for k in (3, 2, 1)]
-        yield
-        receive(flight)
-        small_sum[here_rows, :] = (small_b[...] + land[4]) + (land[5] + land[6])
-        flight = [wire.copy(small_sum.at[here_rows, :], small_sum.at[here_rows, :], here.core())]
-        yield
-        receive(flight)
-        stored.append(local(small_sum, r.small_o))
-        yield
-
-    third = 4 * D // 3
-    early = 2 * FF // EARLY
-    units = [reduce_unit(early * i, early, FORMS[i]) for i in range(EARLY)]
-    units += [reduce_unit(2 * FF + third * i, third, FORMS[EARLY + i]) for i in range(3)]
-    units.append(reduce_small())
-    plan = iter(PLAN)
-
-    def advance():
-        for unit in next(plan):
-            next(units[unit])
 
     started = 0
     for ck in range(2 * chunks):
@@ -520,12 +546,12 @@
             gstt[p, :, qb * QB : (qb + 1) * QB] = jnp.concatenate(filled, axis=0)
         gst[p] = gstt[p].T
     other = pl.multiple_of((1 - here.rows_half) * M, M)
-    dkv_copies = []
+    dkv_out, dkv_in = wire.sender(), [wire.receiver() for _ in range(pairs)]
     gp = r.grad_projected
 
     def finish_pair(p):
         gp[p, :, 0:128] = qgt[p * 128 : (p + 1) * 128, :].T.astype(bf16)
-        dkv_copies[p].wait_recv()
+        take(dkv_in[p], r.land_dkv.at[p])
         gp[p, :, 128:384] = (
             dkv[p, pl.ds(own, M), :].astype(f32) + r.land_dkv[p].astype(f32)
         ).astype(bf16)
@@ -542,8 +568,8 @@
         keys = slice(c * CB, (c + 1) * CB)
         dkv[p, keys, 0:128] = dot_nn(dss[p % 2][keys, :], qst[p]).astype(bf16)
         if c == 3:
-            dkv_copies.append(
-                wire.copy(dkv.at[p, pl.ds(other, M), :], r.land_dkv.at[p], here.core())
+            wire.copy(
+                dkv.at[p, pl.ds(other, M), :], r.land_dkv.at[p], here.core(), dkv_out, dkv_in[p]
             )
 
     def grad_queries(p, qb):
@@ -592,7 +618,6 @@
         r.gtok_stage[rows, :] = grad.astype(bf16)
         if t == 0:
             advance()
-    gtok_copies = send_back(r.gtok_stage, r.gtok_o)
 
     small = r.small
     for k in range(6):
@@ -600,9 +625,15 @@
     small[24:32, :] = acc[8:16, :]
     next(units[EARLY + 3])
     advance()
-    for made in out_copies + gtok_copies:
-        made.wait_recv()
-    wire.finish()
+    take(out_in, r.out_stage)
+    take(gtok_in, r.gtok_stage)
+    take(cotangent_out, r.cotangent_v)
+    take(kv_out, kv.at[:, pl.ds(0, M), :])
+    take(dkv_out, r.land_dkv)
+    take(out_out, r.out_stage)
+    take(gtok_out, r.gtok_stage)
+    take(small_out, r.land_small)
+    take(units_out, arena.at[pl.ds(0, units_rows[0]), :])
     for made in stored:
         made.wait()
 
@@ -610,6 +641,7 @@
 def last_kernel(sizes, names, *refs):
     r = SimpleNamespace(**dict(zip(names, refs, strict=True)))
     D, FF = sizes
+    rows_total = 2 * FF + 4 * D
     sems = r.sems
     count = [0]
 
@@ -619,18 +651,53 @@
         made.start()
         return made
 
-    small_in = local(r.small_i, r.small_i_v)
+    grads_in = []
+    for k in range(rows_total // D):
+        rows = pl.ds(k * D, D)
+        grads_in.append(local(r.grads_i.at[rows, :], r.grads_v.at[rows, :]))
+        if k == 0:
+            small_in = local(r.small_i, r.small_i_v)
+            table_in = local(r.emb_table, r.emb_table_v)
     ada_in = local(r.ada_weight, r.ada_weight_v)
     out_in = local(r.out_i, r.out_i_v)
     gtok_in = local(r.gtok_i, r.gtok_i_v)
-    grads_in = []
-    for b in range(3):
-        rows = pl.ds(b * 4 * D, 4 * D)
-        grads_in.append(local(r.grads_i.at[rows, :], r.grads_v.at[rows, :]))
     outs = []
+    grads = r.grads_v
+
+    def widen(k, target):
+        grads_in[k].wait()
+        target[...] = grads[k * D : (k + 1) * D, :].astype(f32)
+
+    for k in range(FF // D):
+        rows = pl.ds(k * D, D)
+        widen(k, r.gdown_v.at[rows, :])
+        outs.append(local(r.gdown_v.at[rows, :], r.gdown.at[0, rows, :]))
+    for k in range(FF // D):
+        cols = pl.ds(k * D, D)
+        widen(FF // D + k, r.gup_v.at[k])
+        outs.append(local(r.gup_v.at[k], r.gup.at[0, :, cols]))
+    first = 2 * FF // D
+    widen(first, r.gout_v)
+    outs.append(local(r.gout_v, r.gout.at[0]))
+    for p in range(D // 128):
+        grads_in[first + 1 + p].wait()
+        rows = slice((first + 1 + p) * D, (first + 2 + p) * D)
+        for k in range(3):
+            cols = slice(k * D + p * 128, k * D + (p + 1) * 128)
+            r.gqkv_v[:, cols] = grads[rows, k * 128 : (k + 1) * 128].astype(f32)
+    outs.append(local(r.gqkv_v, r.gqkv.at[0]))
+    for arrived, given, wide_v, result in (
+        (out_in, r.out_i_v, r.out_v, r.out),
+        (gtok_in, r.gtok_i_v, r.gtok_v, r.gtok),
+    ):
+        arrived.wait()
+        for s in range(4):
+            wide_v[s] = given[s].astype(f32)
+        outs.append(local(wide_v, result.at[0]))
     small_in.wait()
+    table_in.wait()
     small = r.small_i_v
-    table = r.emb_table[...].astype(f32)
+    table = r.emb_table_v[...].astype(f32)
     sigmoid = 1.0 / (1.0 + jnp.exp(-table))
     silu = table * sigmoid
 
@@ -648,43 +715,17 @@
         block = small[4 * k : 4 * k + 4, :]
         high, low = split(block)
         right = jnp.concatenate([high, high, low, zero], axis=0).astype(bf16)
-        r.gada_v[:, cols] = dot_tn(left, right)
+        r.gada_v[k] = dot_tn(left, right)
+        outs.append(local(r.gada_v.at[k], r.gada.at[0, :, pl.ds(k * D, D)]))
         r.gada_b[:, cols] = col_sum(block)
         both = jnp.concatenate([high, low, zero, zero], axis=0).astype(bf16)
         found = dot_nt(both, r.ada_weight_v[0, :, cols])
         grad_silu = grad_silu + found[0:4, :] + found[4:8, :]
-    outs.append(local(r.gada_v, r.gada.at[0]))
     r.table_o[...] = grad_silu * (sigmoid + table * sigmoid * (1.0 - sigmoid))
     r.down_b[...] = small[24:25, :]
     for k in range(FF // D):
         r.up_b[:, k * D : (k + 1) * D] = small[25 + k : 26 + k, :]
     r.out_b[...] = small[29:30, :]
-    for arrived, given, wide_v, result in (
-        (out_in, r.out_i_v, r.out_v, r.out),
-        (gtok_in, r.gtok_i_v, r.gtok_v, r.gtok),
-    ):
-        arrived.wait()
-        for s in range(4):
-            wide_v[s] = given[s].astype(f32)
-        outs.append(local(wide_v, result.at[0]))
-    grads = r.grads_v
-    grads_in[0].wait()
-    for k in range(FF // D):
-        r.gdown_v[k * D : (k + 1) * D, :] = grads[k * D : (k + 1) * D, :].astype(f32)
-    outs.append(local(r.gdown_v, r.gdown.at[0]))
-    grads_in[1].wait()
-    for k in range(FF // D):
-        r.gup_v[:, k * D : (k + 1) * D] = grads[FF + k * D : FF + (k + 1) * D, :].astype(f32)
-    outs.append(local(r.gup_v, r.gup.at[0]))
-    grads_in[2].wait()
-    r.gout_v[...] = grads[2 * FF : 2 * FF + D, :].astype(f32)
-    outs.append(local(r.gout_v, r.gout.at[0]))
-    for p in range(D // 128):
-        for k in range(3):
-            rows = slice(2 * FF + (p + 1) * D, 2 * FF + (p + 2) * D)
-            cols = slice(k * D + p * 128, k * D + (p + 1) * 128)
-            r.gqkv_v[:, cols] = grads[rows, k * 128 : (k + 1) * 128].astype(f32)
-    outs.append(local(r.gqkv_v, r.gqkv.at[0]))
     for made in outs:
         made.wait()
 
@@ -702,20 +743,25 @@
     arguments = dict(
         tokens=anywhere,
         cotangent=anywhere,
-        emb_table=vmem,
+        emb_table=anywhere,
         ada_weight=anywhere,
-        ada_bias=vmem,
+        ada_bias=anywhere,
         qkv_weight=anywhere,
         out_weight=anywhere,
-        out_bias=vmem,
+        out_bias=anywhere,
         up_weight=anywhere,
-        up_bias=vmem,
+        up_bias=anywhere,
         down_weight=anywhere,
-        down_bias=vmem,
+        down_bias=anywhere,
         lead_class=smem,
         group_count=smem,
     )
     scratch = dict(
+        emb_table_v=pltpu.VMEM(emb_table.shape, bf16),
+        ada_bias_v=pltpu.VMEM((1, 6 * D), bf16),
+        out_bias_v=pltpu.VMEM((1, D), bf16),
+        up_bias_v=pltpu.VMEM((1, FF), bf16),
+        down_bias_v=pltpu.VMEM((1, D), bf16),
         ada_weight_v=pltpu.VMEM((D, 6 * D), bf16),
         qkv_weight_v=pltpu.VMEM((pairs, D, 384), bf16),
         out_weight_v=pltpu.VMEM((D, D), bf16),
@@ -764,10 +810,10 @@
         small_a=pltpu.VMEM((16, D), f32),
         small_b=pltpu.VMEM((16, D), f32),
         small_sum=pltpu.VMEM((32, D), f32),
-        land_small=pltpu.VMEM((7, 16, D), f32),
-        send_sems=pltpu.SemaphoreType.DMA((176,)),
-        recv_sems=pltpu.SemaphoreType.DMA((176,)),
-        local_sems=pltpu.SemaphoreType.DMA((24,)),
+        land_small=pltpu.VMEM((8, 16, D), f32),
+        send_sems=pltpu.SemaphoreType.DMA((8,)),
+        recv_sems=pltpu.SemaphoreType.DMA((69,)),
+        local_sems=pltpu.SemaphoreType.DMA((20,)),
     )
     mids = dict(
         out_o=jax.ShapeDtypeStruct((4, R, D), bf16),
@@ -806,23 +852,24 @@
         gtok_i=anywhere,
         grads_i=anywhere,
         small_i=anywhere,
-        emb_table=vmem,
+        emb_table=anywhere,
         ada_weight=anywhere,
     )
     scratch = dict(
         out_i_v=pltpu.VMEM((4, R, D), bf16),
         gtok_i_v=pltpu.VMEM((4, R, D), bf16),
         grads_v=pltpu.VMEM((total_rows, D), bf16),
+        emb_table_v=pltpu.VMEM(emb_table.shape, bf16),
         small_i_v=pltpu.VMEM((32, D), f32),
         ada_weight_v=pltpu.VMEM((1, D, 6 * D), bf16),
         out_v=pltpu.VMEM((4, R, D), f32),
         gtok_v=pltpu.VMEM((4, R, D), f32),
-        gada_v=pltpu.VMEM((D, 6 * D), f32),
+        gada_v=pltpu.VMEM((6, D, D), f32),
         gqkv_v=pltpu.VMEM((D, 3 * D), f32),
         gout_v=pltpu.VMEM((D, D), f32),
-        gup_v=pltpu.VMEM((D, FF), f32),
+        gup_v=pltpu.VMEM((FF // D, D, D), f32),
         gdown_v=pltpu.VMEM((FF, D), f32),
-        sems=pltpu.SemaphoreType.DMA((16,)),
+        sems=pltpu.SemaphoreType.DMA((40,)),
     )
     names = tuple(ins) + tuple(outs) + tuple(scratch)
     return pl.pallas_call(

time: 96.4 us -> 91.1 us (0.945)
  Pallas kernels: 95.3 us -> 90.1 us
    pallas_call x1, Pallas kernels: 87 us -> 82.2 us  [fast_body(): pl.pallas_call(functools.partial(main_kernel, (R, D, FF), names), out_sha...]
where the time goes in v3:
time: 91.1 us; the launch traced here: 90.9 us
  Pallas kernels  90.1 us (99%)
    pallas_call x1, Pallas kernels, fast_body(): pl.pallas_call(functools.partial(main_kernel, (R, D, FF), names), out_sha...  82.2 us
    pallas_call x1, Pallas kernels, fast_body(): pl.pallas_call(functools.partial(last_kernel, (D, FF), names), out_shape=...  7.93 us

profile of v3, /device:TPU:9, one launch (start us, length us, event | category | flops | bytes accessed | tf_op | source)
XLA Modules:
  0.0 90.9 jit_solution(4080057643735742786)
XLA Ops:
  0.6 82.2 %block_forward_backward.1 = (bf16[4,128,384]{2,1,0:T(8,128)(2,1)}, bf16[4,128,384]{2,1,0:T(8,128)(2,1)}, bf16[4608,384]{1,0:T(8,128)(2,1)}, f32[32,384]{1,0:T(8,128)}) custom-call(bf16[1,4,128,384]{3,2,1,0:T(8,128)(2,1)} %refs_0_.1, bf16[1,4,128,384]{3,2,1,0:T(8,128)(2,1)} %refs_1_.1, bf16[4,384]{1,0:T(4,128)(2,1)} %refs_4_.3, ...), custom_call_target="tpu_custom_call" | custom-call | tf_op jit(solution)/shard_map/block_forward_backward/pallas_call | solution.py:825
  82.8 7.9 %widen_and_embed.1 = (f32[1,4,128,384]{3,2,1,0:T(8,128)}, f32[1,4,128,384]{3,2,1,0:T(8,128)}, f32[4,384]{1,0:T(4,128)}, f32[1,384,2304]{2,1,0:T(8,128)}, f32[1,2...) custom-call(bf16[4,128,384]{2,1,0:T(8,128)(2,1)} %get-tuple-element., ...), custom_call_target="tpu_custom_call" | custom-call | tf_op jit(solution)/shard_map/widen_and_embed/pallas_call | solution.py:875

commit v4 on v3

--- a/solution.py
+++ b/solution.py
@@ -18,8 +18,7 @@
 EARLY = 6
 FORMS = (False, False, False, False, False, False, False, False, False)
 PLAN = (
-    (12, 13, 10, 11),
-    (),
+    (12, 13, 11),
     (),
     (),
     (),
@@ -28,8 +27,8 @@
     (),
     (0,),
     (1, 2),
-    (3, 4, 5),
-    (),
+    (3, 4),
+    (5,),
     (),
     (),
     (),
@@ -40,12 +39,13 @@
     (1,),
     (),
     (),
-    (6, 2),
+    (2, 6),
     (),
     (0, 3),
-    (7, 4, 1),
-    (2,),
-    (5, 15, 8, 0, 6, 9, 3, 4, 7, 1, 2, 5, 8, 6, 0, 3, 9, 0, 4, 7, 1, 5, 1, 8, 2, 14, 16, 6, 2, 3, 9, 3, 7, 9, 4, 8, 4, 17, 5, 5, 6, 6, 7, 7, 8, 8),
+    (),
+    (4, 7, 2, 5, 1),
+    (),
+    (8, 6, 0, 3, 9, 4, 7, 2, 5, 8, 1, 6, 0, 3, 9, 4, 0, 7, 2, 5, 8, 14, 17, 2, 1, 6, 1, 10, 3, 9, 7, 3, 9, 4, 8, 16, 4, 15, 5, 5, 6, 6, 7, 7, 8, 8),
 )
 
 
@@ -308,9 +308,8 @@
     for p in range(pairs):
         att[:, p * 128 : (p + 1) * 128] = ots[p * 128 : (p + 1) * 128, :].T.astype(bf16)
 
-    part, total, arena = r.part, r.total, r.arena
+    part, total, arena = r.part, r.grads_o, r.arena
     used = [0]
-    stored = []
 
     def room(rows):
         start = used[0]
@@ -389,8 +388,6 @@
         move(total.at[keep, :], total.at[keep, :], here.core(), arrived)
         yield
         take(arrived, total.at[pl.ds(0, half), :])
-        keep = pl.ds(base, rows)
-        stored.append(local(total.at[keep, :], r.grads_o.at[keep, :]))
         yield
 
     small_out = wire.sender()
@@ -401,7 +398,7 @@
             r.small_a,
             r.small_b,
             r.land_small,
-            r.small_sum,
+            r.small_o,
         )
         here_rows = span(0, here.c, 16)
         arrived = wire.receiver()
@@ -427,7 +424,6 @@
         )
         yield
         take(arrived, small_sum.at[pl.ds(0, 16), :])
-        stored.append(local(small_sum, r.small_o))
         yield
 
     def send_back(stage, landing, i, sender, receiver):
@@ -507,8 +503,8 @@
     for _ in range(chunks + 2):
         for block in blocks:
             next(block)
+    take(cotangent_in, r.cotangent_v)
     advance()
-    take(cotangent_in, r.cotangent_v)
     for _ in range(chunks + 3):
         for block in blocks:
             next(block, None)
@@ -625,8 +621,8 @@
     small[24:32, :] = acc[8:16, :]
     next(units[EARLY + 3])
     advance()
-    take(out_in, r.out_stage)
-    take(gtok_in, r.gtok_stage)
+    take(out_in, r.out_o)
+    take(gtok_in, r.gtok_o)
     take(cotangent_out, r.cotangent_v)
     take(kv_out, kv.at[:, pl.ds(0, M), :])
     take(dkv_out, r.land_dkv)
@@ -634,14 +630,11 @@
     take(gtok_out, r.gtok_stage)
     take(small_out, r.land_small)
     take(units_out, arena.at[pl.ds(0, units_rows[0]), :])
-    for made in stored:
-        made.wait()
 
 
 def last_kernel(sizes, names, *refs):
     r = SimpleNamespace(**dict(zip(names, refs, strict=True)))
     D, FF = sizes
-    rows_total = 2 * FF + 4 * D
     sems = r.sems
     count = [0]
 
@@ -651,21 +644,12 @@
         made.start()
         return made
 
-    grads_in = []
-    for k in range(rows_total // D):
-        rows = pl.ds(k * D, D)
-        grads_in.append(local(r.grads_i.at[rows, :], r.grads_v.at[rows, :]))
-        if k == 0:
-            small_in = local(r.small_i, r.small_i_v)
-            table_in = local(r.emb_table, r.emb_table_v)
+    table_in = local(r.emb_table, r.emb_table_v)
     ada_in = local(r.ada_weight, r.ada_weight_v)
-    out_in = local(r.out_i, r.out_i_v)
-    gtok_in = local(r.gtok_i, r.gtok_i_v)
     outs = []
-    grads = r.grads_v
+    grads = r.grads_i
 
     def widen(k, target):
-        grads_in[k].wait()
         target[...] = grads[k * D : (k + 1) * D, :].astype(f32)
 
     for k in range(FF // D):
@@ -680,23 +664,17 @@
     widen(first, r.gout_v)
     outs.append(local(r.gout_v, r.gout.at[0]))
     for p in range(D // 128):
-        grads_in[first + 1 + p].wait()
         rows = slice((first + 1 + p) * D, (first + 2 + p) * D)
         for k in range(3):
             cols = slice(k * D + p * 128, k * D + (p + 1) * 128)
             r.gqkv_v[:, cols] = grads[rows, k * 128 : (k + 1) * 128].astype(f32)
     outs.append(local(r.gqkv_v, r.gqkv.at[0]))
-    for arrived, given, wide_v, result in (
-        (out_in, r.out_i_v, r.out_v, r.out),
-        (gtok_in, r.gtok_i_v, r.gtok_v, r.gtok),
-    ):
-        arrived.wait()
+    for given, wide_v, result in ((r.out_i, r.out_v, r.out), (r.gtok_i, r.gtok_v, r.gtok)):
         for s in range(4):
             wide_v[s] = given[s].astype(f32)
         outs.append(local(wide_v, result.at[0]))
-    small_in.wait()
     table_in.wait()
-    small = r.small_i_v
+    small = r.small_i
     table = r.emb_table_v[...].astype(f32)
     sigmoid = 1.0 / (1.0 + jnp.exp(-table))
     silu = table * sigmoid
@@ -804,32 +782,30 @@
         grad_projected=pltpu.VMEM((pairs, M, 384), bf16),
         gtok_stage=pltpu.VMEM((M, D), bf16),
         part=pltpu.VMEM((total_rows, D), bf16),
-        total=pltpu.VMEM((total_rows, D), bf16),
         arena=pltpu.VMEM((2 * total_rows, D), bf16),
         small=pltpu.VMEM((32, D), f32),
         small_a=pltpu.VMEM((16, D), f32),
         small_b=pltpu.VMEM((16, D), f32),
-        small_sum=pltpu.VMEM((32, D), f32),
         land_small=pltpu.VMEM((8, 16, D), f32),
         send_sems=pltpu.SemaphoreType.DMA((8,)),
         recv_sems=pltpu.SemaphoreType.DMA((69,)),
         local_sems=pltpu.SemaphoreType.DMA((20,)),
     )
     mids = dict(
-        out_o=jax.ShapeDtypeStruct((4, R, D), bf16),
-        gtok_o=jax.ShapeDtypeStruct((4, R, D), bf16),
-        grads_o=jax.ShapeDtypeStruct((total_rows, D), bf16),
-        small_o=jax.ShapeDtypeStruct((32, D), f32),
+        out_o=pltpu.VMEM((4, R, D), bf16),
+        gtok_o=pltpu.VMEM((4, R, D), bf16),
+        grads_o=pltpu.VMEM((total_rows, D), bf16),
+        small_o=pltpu.VMEM((32, D), f32),
     )
     names = tuple(arguments) + tuple(mids) + tuple(scratch)
     middle = pl.pallas_call(
         functools.partial(main_kernel, (R, D, FF), names),
         out_shape=tuple(mids.values()),
         in_specs=list(arguments.values()),
-        out_specs=(anywhere,) * 4,
+        out_specs=(vmem,) * 4,
         scratch_shapes=list(scratch.values()),
         compiler_params=pltpu.CompilerParams(
-            collective_id=0, has_side_effects=True, vmem_limit_bytes=60 << 20
+            collective_id=0, has_side_effects=True, vmem_limit_bytes=58 << 20
         ),
         name="block_forward_backward",
     )(*args)
@@ -848,19 +824,15 @@
         down_b=((1, D), vmem),
     )
     ins = dict(
-        out_i=anywhere,
-        gtok_i=anywhere,
-        grads_i=anywhere,
-        small_i=anywhere,
+        out_i=vmem,
+        gtok_i=vmem,
+        grads_i=vmem,
+        small_i=vmem,
         emb_table=anywhere,
         ada_weight=anywhere,
     )
     scratch = dict(
-        out_i_v=pltpu.VMEM((4, R, D), bf16),
-        gtok_i_v=pltpu.VMEM((4, R, D), bf16),
-        grads_v=pltpu.VMEM((total_rows, D), bf16),
         emb_table_v=pltpu.VMEM(emb_table.shape, bf16),
-        small_i_v=pltpu.VMEM((32, D), f32),
         ada_weight_v=pltpu.VMEM((1, D, 6 * D), bf16),
         out_v=pltpu.VMEM((4, R, D), f32),
         gtok_v=pltpu.VMEM((4, R, D), f32),
@@ -878,7 +850,7 @@
         in_specs=list(ins.values()),
         out_specs=tuple(space for _, space in outs.values()),
         scratch_shapes=list(scratch.values()),
-        compiler_params=pltpu.CompilerParams(vmem_limit_bytes=60 << 20),
+        compiler_params=pltpu.CompilerParams(vmem_limit_bytes=40 << 20),
         name="widen_and_embed",
     )(*middle, emb_table, ada_weight)
 

time: 91.1 us -> 87.3 us (0.958)
  Pallas kernels: 90.1 us -> 86.2 us
    pallas_call x1, Pallas kernels: 7.93 us -> 5.8 us  [fast_body(): pl.pallas_call(functools.partial(last_kernel, (D, FF), names), out_shape=...]
    pallas_call x1, Pallas kernels: 82.2 us -> 80.4 us  [fast_body(): pl.pallas_call(functools.partial(main_kernel, (R, D, FF), names), out_sha...]
where the time goes in v4:
time: 87.3 us; the launch traced here: 87.1 us
  Pallas kernels  86.2 us (99%)
    pallas_call x1, Pallas kernels, fast_body(): pl.pallas_call(functools.partial(main_kernel, (R, D, FF), names), out_sha...  80.4 us
    pallas_call x1, Pallas kernels, fast_body(): pl.pallas_call(functools.partial(last_kernel, (D, FF), names), out_shape=...  5.8 us

profile of v4, /device:TPU:9, one launch (start us, length us, event | category | flops | bytes accessed | tf_op | source)
XLA Modules:
  0.0 87.1 jit_solution(2109347785675524884)
XLA Ops:
  0.6 0.0 copy-start
  0.7 0.0 copy-start.1
  0.7 80.4 %block_forward_backward.1 = (bf16[4,128,384]{2,1,0:T(8,128)(2,1)S(1)}, bf16[4,128,384]{2,1,0:T(8,128)(2,1)S(1)}, bf16[4608,384]{1,0:T(8,128)(2,1)S(1)}, f32[32,384]{1,0:T(8,128)S(1)}) custom-call(bf16[1,4,128,384]{3,2,1,0:T(8,128)(2,1)} %refs_0_.1, bf16[1,4,128,384]{3,2,1,0:T(8,128)(2,1)} %refs_1_.1, bf16[4,384]{1,0:T(4,128)(2,1)} %refs_4_.3, ...), custom_call_target="tpu_custom_call" | custom-call | tf_op jit(solution)/shard_map/block_forward_backward/pallas_call | solution.py:801
  81.1 0.0 copy-done
  81.1 0.0 copy-done.1
  81.1 5.8 %widen_and_embed.1 = (f32[1,4,128,384]{3,2,1,0:T(8,128)}, f32[1,4,128,384]{3,2,1,0:T(8,128)}, f32[4,384]{1,0:T(4,128)}, f32[1,384,2304]{2,1,0:T(8,128)}, f32[1,2...) custom-call(bf16[4,128,384]{2,1,0:T(8,128)(2,1)S(1)} %get-tuple-elem, ...), custom_call_target="tpu_custom_call" | custom-call | tf_op jit(solution)/shard_map/widen_and_embed/pallas_call | solution.py:847
Async XLA Ops:
  0.6 80.5 %copy-start = (bf16[1,384,2304]{2,1,0:T(8,128)(2,1)S(1)}, bf16[1,384,2304]{2,1,0:T(8,128)(2,1)}, u32[]{:S(2)}) copy-start(bf16[1,384,2304]{2,1,0:T(8,128)(2,1)} %refs_5_.3) | copy-start | bytes 5308420
  0.7 80.5 %copy-start.1 = (bf16[4,384]{1,0:T(4,128)(2,1)S(1)}, bf16[4,384]{1,0:T(4,128)(2,1)}, u32[]{:S(2)}) copy-start(bf16[4,384]{1,0:T(4,128)(2,1)} %refs_4_.3) | copy-start | bytes 9220

commit v5 on v4

--- a/solution.py
+++ b/solution.py
@@ -18,7 +18,7 @@
 EARLY = 6
 FORMS = (False, False, False, False, False, False, False, False, False)
 PLAN = (
-    (12, 13, 11),
+    (10, 11, 13),
     (),
     (),
     (),
@@ -34,18 +34,18 @@
     (),
     (),
     (),
+    (),
     (0,),
-    (),
     (1,),
     (),
     (),
+    (),
     (2, 6),
-    (),
-    (0, 3),
-    (),
-    (4, 7, 2, 5, 1),
-    (),
-    (8, 6, 0, 3, 9, 4, 7, 2, 5, 8, 1, 6, 0, 3, 9, 4, 0, 7, 2, 5, 8, 14, 17, 2, 1, 6, 1, 10, 3, 9, 7, 3, 9, 4, 8, 16, 4, 15, 5, 5, 6, 6, 7, 7, 8, 8),
+    (3, 0),
+    (),
+    (7, 1, 4, 2, 5),
+    (),
+    (8, 6, 3, 0, 9, 1, 7, 4, 2, 8, 5, 6, 0, 3, 9, 0, 7, 17, 4, 1, 8, 2, 1, 5, 16, 6, 2, 3, 9, 3, 7, 12, 9, 4, 8, 14, 4, 5, 15, 6, 5, 6, 7, 8, 7, 8),
 )
 
 
@@ -789,7 +789,7 @@
         land_small=pltpu.VMEM((8, 16, D), f32),
         send_sems=pltpu.SemaphoreType.DMA((8,)),
         recv_sems=pltpu.SemaphoreType.DMA((69,)),
-        local_sems=pltpu.SemaphoreType.DMA((20,)),
+        local_sems=pltpu.SemaphoreType.DMA((10,)),
     )
     mids = dict(
         out_o=pltpu.VMEM((4, R, D), bf16),
@@ -841,7 +841,7 @@
         gout_v=pltpu.VMEM((D, D), f32),
         gup_v=pltpu.VMEM((FF // D, D, D), f32),
         gdown_v=pltpu.VMEM((FF, D), f32),
-        sems=pltpu.SemaphoreType.DMA((40,)),
+        sems=pltpu.SemaphoreType.DMA((20,)),
     )
     names = tuple(ins) + tuple(outs) + tuple(scratch)
     return pl.pallas_call(

time: 87.3 us -> 87 us (level)
  no operation moved by 1% of the time
where the time goes in v5:
time: 87 us; the launch traced here: 86.8 us
  Pallas kernels  86 us (99%)
    pallas_call x1, Pallas kernels, fast_body(): pl.pallas_call(functools.partial(main_kernel, (R, D, FF), names), out_sha...  80.4 us
    pallas_call x1, Pallas kernels, fast_body(): pl.pallas_call(functools.partial(last_kernel, (D, FF), names), out_shape=...  5.62 us

profile of v5, /device:TPU:9, one launch (start us, length us, event | category | flops | bytes accessed | tf_op | source)
XLA Modules:
  0.0 86.8 jit_solution(17624935091929074074)
XLA Ops:
  0.6 0.0 copy-start
  0.7 0.0 copy-start.1
  0.7 80.4 %block_forward_backward.1 = (bf16[4,128,384]{2,1,0:T(8,128)(2,1)S(1)}, bf16[4,128,384]{2,1,0:T(8,128)(2,1)S(1)}, bf16[4608,384]{1,0:T(8,128)(2,1)S(1)}, f32[32,384]{1,0:T(8,128)S(1)}) custom-call(bf16[1,4,128,384]{3,2,1,0:T(8,128)(2,1)} %refs_0_.1, bf16[1,4,128,384]{3,2,1,0:T(8,128)(2,1)} %refs_1_.1, bf16[4,384]{1,0:T(4,128)(2,1)} %refs_4_.3, ...), custom_call_target="tpu_custom_call" | custom-call | tf_op jit(solution)/shard_map/block_forward_backward/pallas_call | solution.py:801
  81.0 0.0 copy-done
  81.0 0.0 copy-done.1
  81.1 5.6 %widen_and_embed.1 = (f32[1,4,128,384]{3,2,1,0:T(8,128)}, f32[1,4,128,384]{3,2,1,0:T(8,128)}, f32[4,384]{1,0:T(4,128)}, f32[1,384,2304]{2,1,0:T(8,128)}, f32[1,2...) custom-call(bf16[4,128,384]{2,1,0:T(8,128)(2,1)S(1)} %get-tuple-elem, ...), custom_call_target="tpu_custom_call" | custom-call | tf_op jit(solution)/shard_map/widen_and_embed/pallas_call | solution.py:847
Async XLA Ops:
  0.6 80.4 %copy-start = (bf16[1,384,2304]{2,1,0:T(8,128)(2,1)S(1)}, bf16[1,384,2304]{2,1,0:T(8,128)(2,1)}, u32[]{:S(2)}) copy-start(bf16[1,384,2304]{2,1,0:T(8,128)(2,1)} %refs_5_.3) | copy-start | bytes 5308420
  0.7 80.4 %copy-start.1 = (bf16[4,384]{1,0:T(4,128)(2,1)S(1)}, bf16[4,384]{1,0:T(4,128)(2,1)}, u32[]{:S(2)}) copy-start(bf16[4,384]{1,0:T(4,128)(2,1)} %refs_4_.3) | copy-start | bytes 9220
